TPU v7x, 512 devices: a whole 4x8x8 slice. The times are simulated.
512 devices in a mesh: gz: 64 (over y, x, core), gy: 8 (over z).
Axes of the slice: x: 4, y: 8, z: 8, core: 2. Of those that a mesh axis runs over, the one named last changes fastest.
Arguments:
- log_kappa: float32 [128, 128, 128], P('gz', 'gy'), may hold values from -4 to 4
- misfit_weight: float32 [128, 128, 128], P('gz', 'gy'), may hold values from 0.25 to 2.5
- right_side: float32 [128, 128, 128], P('gz', 'gy'), may hold values from -72 to 72
- lift_gain: float32 [64], replicated, may hold values from -4 to 4
- lift_bias: float32 [64], replicated, may hold values from -3 to 3
- spec_one: float32 [128, 8, 32, 4096], P('gz', 'gy'), may hold values from -1.5 to 1.5
- spec_two: float32 [128, 8, 32, 4096], P('gz', 'gy'), may hold values from -1.5 to 1.5
- local_one: float32 [64, 64], replicated, may hold values from -0.75 to 0.75
- local_two: float32 [64, 64], replicated, may hold values from -0.75 to 0.75
- bias_one: float32 [64], replicated, may hold values from -3 to 3
- bias_two: float32 [64], replicated, may hold values from -3 to 3
- readout: float32 [64], replicated, may hold values from -0.75 to 0.75
Outputs:
- solution: float32 [128, 128, 128], P('gz', 'gy')
- residual: float32 [128, 128, 128], P('gz', 'gy')
All inputs are finite; a program needn't handle non-finite values.
Results may differ from a plain program's by a relative error of at most 0.0017.
Values sent between devices are 32-bit elements; how exact they have to be, the bound alone decides.
A program may use at most 64 MiB of HBM per device.

v0:
```python
import math

import jax
import jax.numpy as jnp
from jax import lax
from jax.sharding import PartitionSpec as P

KX = 32
KY = 32
KZ = 32
ITERS = 2


HIGHEST = lax.Precision.HIGHEST
DAMPING = 0.3


def basis_table(modes, length):
    mode_index = jnp.arange(modes, dtype=jnp.int32)
    cell_index = jnp.arange(length, dtype=jnp.int32)
    frequency = (mode_index + 1) // 2
    phase_steps = frequency[:, None] * cell_index[None, :] % length
    angles = phase_steps.astype(jnp.float32) * (2.0 * math.pi / length)
    is_sine = (mode_index % 2 == 0) & (mode_index > 0)
    scales = jnp.where(mode_index == 0, math.sqrt(1.0 / length), math.sqrt(2.0 / length)).astype(
        jnp.float32
    )
    return jnp.where(is_sine[:, None], jnp.sin(angles), jnp.cos(angles)) * scales[:, None]


def gelu_parts(grid_field):
    normal_cdf = 0.5 * (1.0 + lax.erf(grid_field * (1.0 / math.sqrt(2.0))))
    density = jnp.exp(-0.5 * grid_field * grid_field) * (1.0 / math.sqrt(2.0 * math.pi))
    return (grid_field * normal_cdf, normal_cdf + grid_field * density)


def expand(vector):
    return vector[:, None, None, None]


def local_mix(matrix, grid_field):
    return jnp.einsum("io,izyx->ozyx", matrix, grid_field, precision=HIGHEST)


def local_back(matrix, grid_field):
    return jnp.einsum("io,ozyx->izyx", matrix, grid_field, precision=HIGHEST)


def to_modes(grid_field, tables):
    table_x, table_y, table_z = tables
    channels = grid_field.shape[0]
    partial_value = jnp.einsum("czyx,irx->zyric", grid_field, table_x, precision=HIGHEST)
    plane_count, row_count, group_count, freq_count, unused_dim = partial_value.shape
    partial_value = partial_value.reshape(
        plane_count, row_count, group_count, freq_count * channels
    )
    spectra = jnp.einsum(
        "zyq,ky->zkq",
        lax.all_to_all(partial_value, "gy", split_axis=2, concat_axis=1, tiled=True)[:, :, 0, :],
        table_y,
        precision=HIGHEST,
    )
    spectra = spectra.reshape(plane_count, lax.axis_size("gz"), -1)
    planes = lax.all_to_all(spectra, "gz", split_axis=1, concat_axis=0, tiled=True)
    planes = planes.reshape(planes.shape[0], -1)
    return jnp.dot(table_z, planes, precision=HIGHEST)


def to_cells(spectra, tables, channels):
    table_x, table_y, table_z = tables
    planes = jnp.dot(table_z.T, spectra, precision=HIGHEST)
    planes = planes.reshape(planes.shape[0], 1, -1)
    slab_data = lax.all_to_all(planes, "gz", split_axis=0, concat_axis=1, tiled=True)
    plane_count = slab_data.shape[0]
    slab_data = slab_data.reshape(plane_count, table_y.shape[0], -1)
    row_data = jnp.einsum("zkq,ky->zyq", slab_data, table_y, precision=HIGHEST)
    row_data = row_data.reshape(plane_count, row_data.shape[1], 1, -1)
    row_data = lax.all_to_all(row_data, "gy", split_axis=1, concat_axis=2, tiled=True)
    group_count = row_data.shape[2]
    row_data = row_data.reshape(plane_count, row_data.shape[1], group_count, -1, channels)
    return jnp.einsum("zyric,irx->czyx", row_data, table_x, precision=HIGHEST)


def mode_matrices(weights, channels):
    mode_parts = weights.shape[0]
    return weights.reshape(mode_parts, weights.shape[2], channels, channels)


def mix_forward(spectra, matrices):
    mode_parts, mode_count, channels, unused_dim = matrices.shape
    coeffs = spectra.reshape(mode_count, mode_parts, channels)
    return jnp.einsum("kpi,pkio->kpo", coeffs, matrices, precision=HIGHEST).reshape(mode_count, -1)


def mix_adjoint(spectra, matrices):
    mode_parts, mode_count, channels, unused_dim = matrices.shape
    coeffs = spectra.reshape(mode_count, mode_parts, channels)
    return jnp.einsum("kpo,pkio->kpi", coeffs, matrices, precision=HIGHEST).reshape(mode_count, -1)


def local(
    log_kappa,
    misfit_weight,
    right_side,
    lift_gain,
    lift_bias,
    spec_one,
    spec_two,
    local_one,
    local_two,
    bias_one,
    bias_two,
    readout,
):
    channels = lift_gain.shape[0]
    depth_cells, row_cells, line_cells = log_kappa.shape
    group_count = lax.axis_size("gy")
    table_x = basis_table(KX, line_cells).reshape(KX // group_count, group_count, line_cells)
    table_y = basis_table(KY, row_cells * group_count)
    table_z = basis_table(KZ, depth_cells * lax.axis_size("gz"))
    tables = (table_x, table_y, table_z)
    matrices_one = mode_matrices(spec_one, channels)
    matrices_two = mode_matrices(spec_two, channels)
    lift_local = jnp.dot(lift_gain, local_one, precision=HIGHEST)
    bias_local = jnp.dot(lift_bias, local_one, precision=HIGHEST)
    lifted = expand(lift_gain) * log_kappa[None] + expand(lift_bias)
    spectral_in = to_cells(mix_forward(to_modes(lifted, tables), matrices_one), tables, channels)
    pre_one = (
        spectral_in + expand(lift_local) * log_kappa[None] + expand(bias_local) + expand(bias_one)
    )
    act_one, slope_one = gelu_parts(pre_one)
    spectral_two = to_cells(mix_forward(to_modes(act_one, tables), matrices_two), tables, channels)
    pre_two = spectral_two + local_mix(local_two, act_one) + expand(bias_two)
    unused_act, slope_two = gelu_parts(pre_two)

    def residual_sum(values):
        return lax.psum(jnp.sum(values * values), ("gz", "gy"))

    solution = jnp.zeros_like(right_side)
    residual = right_side
    direction = right_side
    norm_now = residual_sum(residual)
    for iteration in range(ITERS):
        lifted_dir = expand(lift_gain) * direction[None]
        spectral_dir = to_cells(
            mix_forward(to_modes(lifted_dir, tables), matrices_one), tables, channels
        )
        tangent_one = slope_one * (spectral_dir + expand(lift_local) * direction[None])
        spectral_mid = to_cells(
            mix_forward(to_modes(tangent_one, tables), matrices_two), tables, channels
        )
        tangent_two = slope_two * (spectral_mid + local_mix(local_two, tangent_one))
        predicted = jnp.einsum("c,czyx->zyx", readout, tangent_two, precision=HIGHEST)
        weighted = misfit_weight * predicted
        back_two = slope_two * (expand(readout) * weighted[None])
        spectral_back = to_cells(
            mix_adjoint(to_modes(back_two, tables), matrices_two), tables, channels
        )
        back_one = slope_one * (spectral_back + local_back(local_two, back_two))
        spectral_zero = to_cells(
            mix_adjoint(to_modes(back_one, tables), matrices_one), tables, channels
        )
        grad_zero = spectral_zero + local_back(local_one, back_one)
        pulled = jnp.einsum("c,czyx->zyx", lift_gain, grad_zero, precision=HIGHEST)
        applied = pulled + DAMPING * direction
        curvature = lax.psum(jnp.sum(direction * applied), ("gz", "gy"))
        applied, curvature = (applied, curvature)
        step_size = norm_now / curvature
        solution = solution + step_size * direction
        residual = residual - step_size * applied
        norm_next = residual_sum(residual)
        direction = residual + norm_next / norm_now * direction
        norm_now = norm_next
    return (solution, residual)


def solution(mesh):
    return jax.shard_map(
        local,
        mesh=mesh,
        in_specs=(
            P("gz", "gy", None),
            P("gz", "gy", None),
            P("gz", "gy", None),
            P(),
            P(),
            P("gz", "gy", None, None),
            P("gz", "gy", None, None),
            P(),
            P(),
            P(),
            P(),
            P(),
        ),
        out_specs=(P("gz", "gy", None), P("gz", "gy", None)),
        check_vma=False,
    )
```

profile of v0, /device:TPU:1, one launch (start us, length us, event | category | flops | bytes accessed | tf_op | source)
XLA Modules:
  0.0 1013.4 jit_solution(15844240353886195524)
XLA Ops:
  5.9 10.9 %all-to-all-start = ((f32[2,16,8,256]{3,1,0,2:T(8,128)}), f32[2,16,8,256]{3,1,0,2:T(8,128)S(1)}, u32[]{:S(2)}, u32[]{:S(2)}) async-start(f32[2,16,8,256]{3,1,0,2:T(8,128)} %reshape.523), calls=%async_computation | async-start | bytes 524288 | tf_op jit(solution)/shard_map/all_to_all | solution.py:59
  39.9 13.6 %all-to-all-start.1 = ((f32[2,64,128]{2,0,1:T(2,128)}), f32[2,64,128]{2,0,1:T(2,128)S(1)}, u32[]{:S(2)}, u32[]{:S(2)}) async-start(f32[2,64,128]{2,0,1:T(2,128)} %copy.186), calls=%async_computation.1 | async-start | bytes 131072 | tf_op jit(solution)/shard_map/all_to_all | solution.py:64
  112.7 10.4 %all-to-all-done.3 = f32[2,128,1,256]{3,0,2,1:T(2,128)S(1)} async-done(((f32[2,128,1,256]{3,0,2,1:T(2,128)}), f32[2,128,1,256]{3,0,2,1:T(2,128)S(1)}, u32[]{:S(2)}, u32[]{:S(2)}) %all-to-all-start.3) | async-done | bytes 262176 | tf_op jit(solution)/shard_map/all_to_all | solution.py:78
  180.5 9.0 all-to-all-done.5
  240.0 10.7 %all-to-all-done.7 = f32[2,128,1,256]{3,0,2,1:T(2,128)S(1)} async-done(((f32[2,128,1,256]{3,0,2,1:T(2,128)}), f32[2,128,1,256]{3,0,2,1:T(2,128)S(1)}, u32[]{:S(2)}, u32[]{:S(2)}) %all-to-all-start.7) | async-done | bytes 262176 | tf_op jit(solution)/shard_map/all_to_all | solution.py:78
  279.0 13.1 %all_to_all.600 = f32[2,16,8,256]{3,1,0,2:T(8,128)S(1)} all-to-all(f32[2,16,8,256]{3,1,0,2:T(8,128)S(1)} %reshape.527), channel_id=1, replica_groups=mesh['gz'=64,'gy'=8] {'gy'}, dimensions={2} | all-to-all | bytes 524288 | tf_op jit(solution)/shard_map/all_to_all | solution.py:59
  292.5 16.1 %all_to_all.601 = f32[2,64,128]{2,0,1:T(2,128)S(1)} all-to-all(f32[2,64,128]{2,0,1:T(2,128)S(1)} %copy.228), channel_id=1, replica_groups=mesh['gz'=64,'gy'=8] {'gz'}, dimensions={1} | all-to-all | bytes 131072 | tf_op jit(solution)/shard_map/all_to_all | solution.py:64
  314.5 13.8 %all_to_all.602 = f32[128,1,128]{2,1,0:T(1,128)S(1)} all-to-all(f32[128,1,128]{2,1,0:T(1,128)S(1)} %bitcast.897), channel_id=1, replica_groups=mesh['gz'=64,'gy'=8] {'gz'}, dimensions={0} | all-to-all | bytes 131072 | tf_op jit(solution)/shard_map/all_to_all | solution.py:73
  329.1 14.7 %all_to_all.603 = f32[2,128,1,256]{3,0,2,1:T(2,128)S(1)} all-to-all(f32[2,128,1,256]{3,0,2,1:T(2,128)S(1)} %copy.232), channel_id=1, replica_groups=mesh['gz'=64,'gy'=8] {'gy'}, dimensions={1} | all-to-all | bytes 524288 | tf_op jit(solution)/shard_map/all_to_all | solution.py:78
  355.8 14.5 %all_to_all.604 = f32[2,16,8,256]{3,1,0,2:T(8,128)S(1)} all-to-all(f32[2,16,8,256]{3,1,0,2:T(8,128)S(1)} %reshape.528), channel_id=1, replica_groups=mesh['gz'=64,'gy'=8] {'gy'}, dimensions={2} | all-to-all | bytes 524288 | tf_op jit(solution)/shard_map/all_to_all | solution.py:59
  370.8 14.4 %all_to_all.605 = f32[2,64,128]{2,0,1:T(2,128)S(1)} all-to-all(f32[2,64,128]{2,0,1:T(2,128)S(1)} %copy.238), channel_id=1, replica_groups=mesh['gz'=64,'gy'=8] {'gz'}, dimensions={1} | all-to-all | bytes 131072 | tf_op jit(solution)/shard_map/all_to_all | solution.py:64
  389.6 13.8 %all_to_all.606 = f32[128,1,128]{2,1,0:T(1,128)S(1)} all-to-all(f32[128,1,128]{2,1,0:T(1,128)S(1)} %bitcast.899), channel_id=1, replica_groups=mesh['gz'=64,'gy'=8] {'gz'}, dimensions={0} | all-to-all | bytes 131072 | tf_op jit(solution)/shard_map/all_to_all | solution.py:73
  404.1 14.7 %all_to_all.607 = f32[2,128,1,256]{3,0,2,1:T(2,128)S(1)} all-to-all(f32[2,128,1,256]{3,0,2,1:T(2,128)S(1)} %copy.242), channel_id=1, replica_groups=mesh['gz'=64,'gy'=8] {'gy'}, dimensions={1} | all-to-all | bytes 524288 | tf_op jit(solution)/shard_map/all_to_all | solution.py:78
  425.4 94.0 %all-reduce = (f32[]{:T(128)}, f32[]{:T(128)}) all-reduce(f32[]{:T(128)} %get-tuple-element.3, f32[]{:T(128)} %get-tuple-element.2), channel_id=1, replica_groups=mesh['gz'=64,'gy'=8] {'gz','gy'}, use_global_device_ids=true, to_apply=%region_1.2 | all-reduce | flops 2 | bytes 16 | tf_op jit(solution)/shard_map/psum | solution.py:137
  521.4 94.6 %psum.30 = f32[]{:T(128)} all-reduce(f32[]{:T(128)} %multiply_reduce_fusion.1), channel_id=1, replica_groups=mesh['gz'=64,'gy'=8] {'gz','gy'}, use_global_device_ids=true, to_apply=%region_5.6 | all-reduce | flops 1 | bytes 8 | tf_op jit(solution)/shard_map/psum | solution.py:137
  622.9 13.7 %all_to_all.608 = f32[2,16,8,256]{3,1,0,2:T(8,128)S(1)} all-to-all(f32[2,16,8,256]{3,1,0,2:T(8,128)S(1)} %reshape.529), channel_id=1, replica_groups=mesh['gz'=64,'gy'=8] {'gy'}, dimensions={2} | all-to-all | bytes 524288 | tf_op jit(solution)/shard_map/all_to_all | solution.py:59
  637.0 18.7 %all_to_all.609 = f32[2,64,128]{2,0,1:T(2,128)S(1)} all-to-all(f32[2,64,128]{2,0,1:T(2,128)S(1)} %copy.248), channel_id=1, replica_groups=mesh['gz'=64,'gy'=8] {'gz'}, dimensions={1} | all-to-all | bytes 131072 | tf_op jit(solution)/shard_map/all_to_all | solution.py:64
  658.6 13.8 %all_to_all.610 = f32[128,1,128]{2,1,0:T(1,128)S(1)} all-to-all(f32[128,1,128]{2,1,0:T(1,128)S(1)} %bitcast.901), channel_id=1, replica_groups=mesh['gz'=64,'gy'=8] {'gz'}, dimensions={0} | all-to-all | bytes 131072 | tf_op jit(solution)/shard_map/all_to_all | solution.py:73
  673.2 15.1 %all_to_all.611 = f32[2,128,1,256]{3,0,2,1:T(2,128)S(1)} all-to-all(f32[2,128,1,256]{3,0,2,1:T(2,128)S(1)} %copy.252), channel_id=1, replica_groups=mesh['gz'=64,'gy'=8] {'gy'}, dimensions={1} | all-to-all | bytes 524288 | tf_op jit(solution)/shard_map/all_to_all | solution.py:78
  699.3 14.5 %all_to_all.612 = f32[2,16,8,256]{3,1,0,2:T(8,128)S(1)} all-to-all(f32[2,16,8,256]{3,1,0,2:T(8,128)S(1)} %reshape.530), channel_id=1, replica_groups=mesh['gz'=64,'gy'=8] {'gy'}, dimensions={2} | all-to-all | bytes 524288 | tf_op jit(solution)/shard_map/all_to_all | solution.py:59
  714.3 14.1 %all_to_all.613 = f32[2,64,128]{2,0,1:T(2,128)S(1)} all-to-all(f32[2,64,128]{2,0,1:T(2,128)S(1)} %copy.258), channel_id=1, replica_groups=mesh['gz'=64,'gy'=8] {'gz'}, dimensions={1} | all-to-all | bytes 131072 | tf_op jit(solution)/shard_map/all_to_all | solution.py:64
  732.8 13.8 %all_to_all.614 = f32[128,1,128]{2,1,0:T(1,128)S(1)} all-to-all(f32[128,1,128]{2,1,0:T(1,128)S(1)} %bitcast.903), channel_id=1, replica_groups=mesh['gz'=64,'gy'=8] {'gz'}, dimensions={0} | all-to-all | bytes 131072 | tf_op jit(solution)/shard_map/all_to_all | solution.py:73
  747.4 14.9 %all_to_all.615 = f32[2,128,1,256]{3,0,2,1:T(2,128)S(1)} all-to-all(f32[2,128,1,256]{3,0,2,1:T(2,128)S(1)} %copy.262), channel_id=1, replica_groups=mesh['gz'=64,'gy'=8] {'gy'}, dimensions={1} | all-to-all | bytes 524288 | tf_op jit(solution)/shard_map/all_to_all | solution.py:78
  773.8 14.5 %all_to_all.616 = f32[2,16,8,256]{3,1,0,2:T(8,128)S(1)} all-to-all(f32[2,16,8,256]{3,1,0,2:T(8,128)S(1)} %reshape.531), channel_id=1, replica_groups=mesh['gz'=64,'gy'=8] {'gy'}, dimensions={2} | all-to-all | bytes 524288 | tf_op jit(solution)/shard_map/all_to_all | solution.py:59
  788.7 14.1 %all_to_all.617 = f32[2,64,128]{2,0,1:T(2,128)S(1)} all-to-all(f32[2,64,128]{2,0,1:T(2,128)S(1)} %copy.269), channel_id=1, replica_groups=mesh['gz'=64,'gy'=8] {'gz'}, dimensions={1} | all-to-all | bytes 131072 | tf_op jit(solution)/shard_map/all_to_all | solution.py:64
  808.8 14.1 %all_to_all.618 = f32[128,1,128]{2,1,0:T(1,128)S(1)} all-to-all(f32[128,1,128]{2,1,0:T(1,128)S(1)} %bitcast.905), channel_id=1, replica_groups=mesh['gz'=64,'gy'=8] {'gz'}, dimensions={0} | all-to-all | bytes 131072 | tf_op jit(solution)/shard_map/all_to_all | solution.py:73
  823.7 14.7 %all_to_all.619 = f32[2,128,1,256]{3,0,2,1:T(2,128)S(1)} all-to-all(f32[2,128,1,256]{3,0,2,1:T(2,128)S(1)} %copy.273), channel_id=1, replica_groups=mesh['gz'=64,'gy'=8] {'gy'}, dimensions={1} | all-to-all | bytes 524288 | tf_op jit(solution)/shard_map/all_to_all | solution.py:78
  849.3 14.4 %all_to_all.620 = f32[2,16,8,256]{3,1,0,2:T(8,128)S(1)} all-to-all(f32[2,16,8,256]{3,1,0,2:T(8,128)S(1)} %reshape.532), channel_id=1, replica_groups=mesh['gz'=64,'gy'=8] {'gy'}, dimensions={2} | all-to-all | bytes 524288 | tf_op jit(solution)/shard_map/all_to_all | solution.py:59
  864.1 14.2 %all_to_all.621 = f32[2,64,128]{2,0,1:T(2,128)S(1)} all-to-all(f32[2,64,128]{2,0,1:T(2,128)S(1)} %copy.279), channel_id=1, replica_groups=mesh['gz'=64,'gy'=8] {'gz'}, dimensions={1} | all-to-all | bytes 131072 | tf_op jit(solution)/shard_map/all_to_all | solution.py:64
  882.7 14.1 %all_to_all.622 = f32[128,1,128]{2,1,0:T(1,128)S(1)} all-to-all(f32[128,1,128]{2,1,0:T(1,128)S(1)} %bitcast.907), channel_id=1, replica_groups=mesh['gz'=64,'gy'=8] {'gz'}, dimensions={0} | all-to-all | bytes 131072 | tf_op jit(solution)/shard_map/all_to_all | solution.py:73
  897.7 14.7 %all_to_all.623 = f32[2,128,1,256]{3,0,2,1:T(2,128)S(1)} all-to-all(f32[2,128,1,256]{3,0,2,1:T(2,128)S(1)} %copy.283), channel_id=1, replica_groups=mesh['gz'=64,'gy'=8] {'gy'}, dimensions={1} | all-to-all | bytes 524288 | tf_op jit(solution)/shard_map/all_to_all | solution.py:78
  917.0 94.0 %psum.31 = f32[]{:T(128)} all-reduce(f32[]{:T(128)} %multiply_reduce_fusion), channel_id=1, replica_groups=mesh['gz'=64,'gy'=8] {'gz','gy'}, use_global_device_ids=true, to_apply=%region_7.8 | all-reduce | flops 1 | bytes 8 | tf_op jit(solution)/shard_map/psum | solution.py:166
  (301 shorter events, 321.2 us)
Async XLA Ops:
  0.6 267.7 %copy-start = (f32[64,64]{1,0:T(8,128)S(1)}, f32[64,64]{1,0:T(8,128)}, u32[]{:S(2)}) copy-start(f32[64,64]{1,0:T(8,128)} %param.20) | copy-start | bytes 49156
  0.6 16.1 %copy-start.22 = (f32[64]{0:T(128)S(1)}, f32[64]{0:T(128)}, u32[]{:S(2)}) copy-start(f32[64]{0:T(128)} %param.15) | copy-start | bytes 772
  0.7 16.1 %copy-start.16 = (f32[2,16,128]{2,1,0:T(8,128)S(1)}, f32[2,16,128]{2,1,0:T(8,128)}, u32[]{:S(2)}) copy-start(f32[2,16,128]{2,1,0:T(8,128)} %param.14) | copy-start | bytes 49156
  4.8 25.7 %copy-start.12 = (f32[2,1,32,4096]{3,2,1,0:T(8,128)S(1)}, f32[2,1,32,4096]{3,2,1,0:T(8,128)}, u32[]{:S(2)}) copy-start(f32[2,1,32,4096]{3,2,1,0:T(8,128)} %param.17) | copy-start | bytes 3145732
  5.9 21.2 %all-to-all-start = ((f32[2,16,8,256]{3,1,0,2:T(8,128)}), f32[2,16,8,256]{3,1,0,2:T(8,128)S(1)}, u32[]{:S(2)}, u32[]{:S(2)}) async-start(f32[2,16,8,256]{3,1,0,2:T(8,128)} %reshape.523), calls=%async_computation | async-start | bytes 524288 | tf_op jit(solution)/shard_map/all_to_all | solution.py:59
  27.1 3.4 copy-start.15
  27.1 12.8 %all-to-all-start.8 = ((f32[2,16,8,256]{3,1,0,2:T(8,128)}), f32[2,16,8,256]{3,1,0,2:T(8,128)S(1)}, u32[]{:S(2)}, u32[]{:S(2)}) async-start(f32[2,16,8,256]{3,1,0,2:T(8,128)} %reshape.525), calls=%async_computation.8 | async-start | bytes 524288 | tf_op jit(solution)/shard_map/all_to_all | solution.py:59
  39.9 23.7 %all-to-all-start.1 = ((f32[2,64,128]{2,0,1:T(2,128)}), f32[2,64,128]{2,0,1:T(2,128)S(1)}, u32[]{:S(2)}, u32[]{:S(2)}) async-start(f32[2,64,128]{2,0,1:T(2,128)} %copy.186), calls=%async_computation.1 | async-start | bytes 131072 | tf_op jit(solution)/shard_map/all_to_all | solution.py:64
  63.6 14.5 %all-to-all-start.9 = ((f32[2,64,128]{2,0,1:T(2,128)}), f32[2,64,128]{2,0,1:T(2,128)S(1)}, u32[]{:S(2)}, u32[]{:S(2)}) async-start(f32[2,64,128]{2,0,1:T(2,128)} %copy.207), calls=%async_computation.9 | async-start | bytes 131072 | tf_op jit(solution)/shard_map/all_to_all | solution.py:64
  78.1 14.8 %all-to-all-start.2 = ((f32[128,1,128]{2,1,0:T(1,128)}), f32[128,1,128]{2,1,0:T(1,128)S(1)}, u32[]{:S(2)}, u32[]{:S(2)}) async-start(f32[128,1,128]{2,1,0:T(1,128)} %bitcast.21), calls=%async_computation.2 | async-start | bytes 131072 | tf_op jit(solution)/shard_map/all_to_all | solution.py:73
  83.2 27.7 %copy-start.17 = (f32[64,64]{1,0:T(8,128)S(1)}, f32[64,64]{1,0:T(8,128)}, u32[]{:S(2)}) copy-start(f32[64,64]{1,0:T(8,128)} %param.19) | copy-start | bytes 49156
  83.2 27.7 %copy-start.24 = (f32[64]{0:T(128)S(1)}, f32[64]{0:T(128)}, u32[]{:S(2)}) copy-start(f32[64]{0:T(128)} %param.16) | copy-start | bytes 772
  92.9 14.6 %all-to-all-start.10 = ((f32[128,1,128]{2,1,0:T(1,128)}), f32[128,1,128]{2,1,0:T(1,128)S(1)}, u32[]{:S(2)}, u32[]{:S(2)}) async-start(f32[128,1,128]{2,1,0:T(1,128)} %bitcast.77), calls=%async_computation.10 | async-start | bytes 131072 | tf_op jit(solution)/shard_map/all_to_all | solution.py:73
  98.0 29.8 %copy-start.25 = (f32[2,16,128]{2,1,0:T(8,128)S(1)}, f32[2,16,128]{2,1,0:T(8,128)}, u32[]{:S(2)}) copy-start(f32[2,16,128]{2,1,0:T(8,128)} %param.12) | copy-start | bytes 49156
  98.0 29.8 %copy-start.26 = (f32[64]{0:T(128)S(1)}, f32[64]{0:T(128)}, u32[]{:S(2)}) copy-start(f32[64]{0:T(128)} %param.21) | copy-start | bytes 772
  107.5 15.7 %all-to-all-start.3 = ((f32[2,128,1,256]{3,0,2,1:T(2,128)}), f32[2,128,1,256]{3,0,2,1:T(2,128)S(1)}, u32[]{:S(2)}, u32[]{:S(2)}) async-start(f32[2,128,1,256]{3,0,2,1:T(2,128)} %copy.190), calls=%async_computation.3 | async-start | bytes 524288 | tf_op jit(solution)/shard_map/all_to_all | solution.py:78
  111.2 36.3 %copy-start.23 = (f32[64]{0:T(128)}, f32[64]{0:T(128)S(1)}, u32[]{:S(2)}) copy-start(f32[64]{0:T(128)S(1)} %convolution_bitcast_fusion.58) | copy-start | bytes 772
  123.2 15.3 %all-to-all-start.11 = ((f32[2,128,1,256]{3,0,2,1:T(2,128)}), f32[2,128,1,256]{3,0,2,1:T(2,128)S(1)}, u32[]{:S(2)}, u32[]{:S(2)}) async-start(f32[2,128,1,256]{3,0,2,1:T(2,128)} %copy.211), calls=%async_computation.11 | async-start | bytes 524288 | tf_op jit(solution)/shard_map/all_to_all | solution.py:78
  131.1 16.4 %copy-start.1 = (f32[64,2,16,128]{3,0,2,1:T(8,128)}, f32[64,2,16,128]{3,0,2,1:T(8,128)S(1)}, u32[]{:S(2)}) copy-start(f32[64,2,16,128]{3,0,2,1:T(8,128)S(1)} %get-tuple-element.8) | copy-start | bytes 3145732
  138.5 6.9 copy-start.14
  138.5 17.4 %all-to-all-start.4 = ((f32[2,16,8,256]{3,1,0,2:T(8,128)}), f32[2,16,8,256]{3,1,0,2:T(8,128)}, u32[]{:S(2)}, u32[]{:S(2)}) async-start(f32[2,16,8,256]{3,1,0,2:T(8,128)} %reshape.524), calls=%async_computation.4 | async-start | bytes 524288 | tf_op jit(solution)/shard_map/all_to_all | solution.py:59
  155.9 16.4 %all-to-all-start.12 = ((f32[2,16,8,256]{3,1,0,2:T(8,128)}), f32[2,16,8,256]{3,1,0,2:T(8,128)S(1)}, u32[]{:S(2)}, u32[]{:S(2)}) async-start(f32[2,16,8,256]{3,1,0,2:T(8,128)} %reshape.526), calls=%async_computation.12 | async-start | bytes 524288 | tf_op jit(solution)/shard_map/all_to_all | solution.py:59
  172.3 17.2 %all-to-all-start.5 = ((f32[2,64,128]{2,0,1:T(2,128)}), f32[2,64,128]{2,0,1:T(2,128)S(1)}, u32[]{:S(2)}, u32[]{:S(2)}) async-start(f32[2,64,128]{2,0,1:T(2,128)} %copy.196), calls=%async_computation.5 | async-start | bytes 131072 | tf_op jit(solution)/shard_map/all_to_all | solution.py:64
  189.6 14.5 %all-to-all-start.13 = ((f32[2,64,128]{2,0,1:T(2,128)}), f32[2,64,128]{2,0,1:T(2,128)S(1)}, u32[]{:S(2)}, u32[]{:S(2)}) async-start(f32[2,64,128]{2,0,1:T(2,128)} %copy.217), calls=%async_computation.13 | async-start | bytes 131072 | tf_op jit(solution)/shard_map/all_to_all | solution.py:64
  204.1 15.6 %all-to-all-start.6 = ((f32[128,1,128]{2,1,0:T(1,128)}), f32[128,1,128]{2,1,0:T(1,128)S(1)}, u32[]{:S(2)}, u32[]{:S(2)}) async-start(f32[128,1,128]{2,1,0:T(1,128)} %bitcast.50), calls=%async_computation.6 | async-start | bytes 131072 | tf_op jit(solution)/shard_map/all_to_all | solution.py:73
  219.7 15.4 %all-to-all-start.14 = ((f32[128,1,128]{2,1,0:T(1,128)}), f32[128,1,128]{2,1,0:T(1,128)S(1)}, u32[]{:S(2)}, u32[]{:S(2)}) async-start(f32[128,1,128]{2,1,0:T(1,128)} %bitcast.102), calls=%async_computation.14 | async-start | bytes 131072 | tf_op jit(solution)/shard_map/all_to_all | solution.py:73
  235.1 15.7 %all-to-all-start.7 = ((f32[2,128,1,256]{3,0,2,1:T(2,128)}), f32[2,128,1,256]{3,0,2,1:T(2,128)S(1)}, u32[]{:S(2)}, u32[]{:S(2)}) async-start(f32[2,128,1,256]{3,0,2,1:T(2,128)} %copy.200), calls=%async_computation.7 | async-start | bytes 524288 | tf_op jit(solution)/shard_map/all_to_all | solution.py:78
  250.7 15.3 %all-to-all-start.15 = ((f32[2,128,1,256]{3,0,2,1:T(2,128)}), f32[2,128,1,256]{3,0,2,1:T(2,128)S(1)}, u32[]{:S(2)}, u32[]{:S(2)}) async-start(f32[2,128,1,256]{3,0,2,1:T(2,128)} %copy.221), calls=%async_computation.15 | async-start | bytes 524288 | tf_op jit(solution)/shard_map/all_to_all | solution.py:78
  254.5 13.8 %copy-start.27 = (f32[64]{0:T(128)S(1)}, f32[64]{0:T(128)}, u32[]{:S(2)}) copy-start(f32[64]{0:T(128)} %param.22) | copy-start | bytes 772
  268.4 3.3 copy-start.9
  420.1 3.0 copy-start.7
  896.9 17.8 %copy-start.5 = (f32[64,2,16,128]{3,0,2,1:T(8,128)S(1)}, f32[64,2,16,128]{3,0,2,1:T(8,128)}, u32[]{:S(2)}) copy-start(f32[64,2,16,128]{3,0,2,1:T(8,128)} %copy-done.4) | copy-start | bytes 3145732
  (12 other events, 21.6 us)
where the time goes:
time: 1020 us; the launch traced here: 1010 us
  blocking collectives  631 us (62%)
  matrix products  125 us (12%)
  waiting for transfers between devices  105 us (10%)
  starting transfers between devices  91 us (9%)
  local copies, waits for them, and re-layouts  52.1 us (5%)
    psum x2, blocking collectives, residual_sum(): return lax.psum(jnp.sum(values * values), ('gz', 'gy'))  189 us
    psum x1, blocking collectives, local(): curvature = lax.psum(jnp.sum(direction * applied), ('gz', 'gy'))  94 us
    all_to_all x6, blocking collectives, to_modes(): lax.all_to_all(spectra, 'gz', split_axis=1, concat_axis=0, tiled=True)  91.6 us
    all_to_all x6, blocking collectives, to_cells(): lax.all_to_all(row_data, 'gy', split_axis=1, concat_axis=2, tiled=True)  89 us
    all_to_all x6, blocking collectives, to_modes(): lax.all_to_all(partial_value, 'gy', split_axis=2, concat_axis=1, tiled=True)  84.6 us
    all_to_all x6, blocking collectives, to_cells(): lax.all_to_all(planes, 'gz', split_axis=0, concat_axis=1, tiled=True)  83.3 us
    dot_general x10, matrix products, to_modes(): jnp.einsum('czyx,irx->zyric', grid_field, table_x, precision=HIGHEST)  30.6 us
    all_to_all x4, waiting for transfers between devices, to_cells(): lax.all_to_all(row_data, 'gy', split_axis=1, concat_axis=2, tiled=True)  29.9 us
  transfers between devices with their start and end apart: 16, of which 15 were waited for; matrix products, arithmetic and copies ran while one was open for 6% of the time, Pallas kernels for 0%

commit v1 on v0

v1 whole, which is shorter than its diff:
```python
import functools
import math

import jax
import jax.numpy as jnp
import ml_dtypes
import numpy as np
from jax import lax
from jax.experimental import pallas as pl
from jax.experimental.pallas import tpu as pltpu
from jax.sharding import PartitionSpec as P

KX = 32
KY = 32
KZ = 32
DAMPING = 0.3
HIGHEST = lax.Precision.HIGHEST
MESH = pl.DeviceIdType.MESH
NT = (((1,), (1,)), ((), ()))
UNITS = 15
B0K, B0R, C0A, C0T, D0A, D0T, E0, F0, G0, B1, C1, D1, E1, F1, G1 = range(UNITS)
SUMS = {E0: 0, C1: 1, E1: 2}
UNROLL = 2


def basis_table(modes, length):
    mode_index = np.arange(modes)
    frequency = (mode_index + 1) // 2
    phase_steps = frequency[:, None] * np.arange(length)[None, :] % length
    angles = phase_steps * (2.0 * math.pi / length)
    is_sine = (mode_index % 2 == 0) & (mode_index > 0)
    scales = np.where(mode_index == 0, math.sqrt(1.0 / length), math.sqrt(2.0 / length))
    return (np.where(is_sine[:, None], np.sin(angles), np.cos(angles)) * scales[:, None]).astype(np.float32)


def parts_of(table):
    high = table.astype(ml_dtypes.bfloat16)
    low = (table - high.astype(np.float32)).astype(ml_dtypes.bfloat16)
    return high, low


def wide(table):
    high, low = parts_of(table)
    return np.concatenate([high, low, high], axis=1)


class Sizes:
    def __init__(self, gz, gy, rows, line, kx, ky, kz):
        self.gz, self.gy, self.rows, self.line = gz, gy, rows, line
        self.kx, self.ky, self.kz = kx, ky, kz
        self.kxhi = kx // gy
        self.modes = ky * self.kxhi // gz * kz


def tables_of(s):
    bx, by, bz = basis_table(s.kx, s.line), basis_table(s.ky, s.rows * s.gy), basis_table(s.kz, 2 * s.gz)
    order = np.arange(s.kx).reshape(s.kxhi, s.gy).T.reshape(-1)
    tx = bx[order]
    eye = np.eye(s.kxhi, dtype=np.float32)
    ty = np.einsum("kY,ab->kabY", by, eye).reshape(s.ky * s.kxhi, s.kxhi * s.rows * s.gy)
    byd = by.reshape(s.ky, s.gy, s.rows)
    tyt = np.einsum("kdy,ab->dayKb".replace("K", "k"), byd, eye).reshape(s.gy * s.kxhi * s.rows, s.ky * s.kxhi)
    bzg = bz.reshape(s.kz, s.gz, 2)
    two = np.eye(2, dtype=np.float32)
    tz = np.einsum("kgz,ij->izkgj", bzg, two).reshape(4 * s.kz, 2 * s.gz)
    tza = np.einsum("kgz,ij->izkgj", bzg, np.eye(2, 4, dtype=np.float32)).reshape(4 * s.kz, 4 * s.gz)
    ma = np.zeros((s.gy, 2, 2, s.rows, s.ky, 2, 2), np.float32)
    for f in range(2):
        for z in range(2):
            ma[:, f, z, :, :, z, f] = byd.transpose(1, 2, 0)
    ma = ma.reshape(s.gy, 4 * s.rows, 4 * s.ky)
    full = np.zeros((s.gy, 128, 128), np.float32)
    full[:, : 4 * s.rows, : 4 * s.ky] = ma
    ym = np.broadcast_to(byd.transpose(1, 0, 2)[:, :, None, None, None, :], (s.gy, s.ky, s.kxhi, s.kxhi, 2, s.rows))
    ym = np.ascontiguousarray(ym).reshape(s.gy, s.ky * s.kxhi, s.kxhi * 2 * s.rows)
    lanes = np.arange(128)
    expand = (np.arange(128)[None, :, None] % 64 == 2 * np.arange(32)[:, None, None] + lanes[None, None, :] // 64)
    return [
        tx,
        bx.reshape(s.kxhi, s.gy, s.line),
        wide(tx),
        wide(np.ascontiguousarray(tx.T)),
        wide(ty),
        wide(tyt),
        wide(tz),
        wide(np.ascontiguousarray(tz.T)),
        tza,
        full,
        ym,
        expand.astype(ml_dtypes.bfloat16),
    ]


def split(x):
    high = x.astype(jnp.bfloat16)
    return high, (x - high.astype(jnp.float32)).astype(jnp.bfloat16)


def tall3(x):
    high, low = split(x)
    return jnp.concatenate([high, high, low], axis=0)


def flat3(x):
    high, low = split(x)
    return jnp.concatenate([high, high, low], axis=1)


def dot(a, b):
    return jnp.dot(a, b, preferred_element_type=jnp.float32)


def gelu_parts(grid_field):
    normal_cdf = 0.5 * (1.0 + lax.erf(grid_field * (1.0 / math.sqrt(2.0))))
    density = jnp.exp(-0.5 * grid_field * grid_field) * (1.0 / math.sqrt(2.0 * math.pi))
    return (grid_field * normal_cdf, normal_cdf + grid_field * density)


def total(x):
    return jnp.sum(jnp.sum(x, axis=0, keepdims=True), axis=1, keepdims=True)


def kernel(s, *refs):
    (kappa, weight, rhs, vec, gexp, w1, w2, mats,
     tx, txk, tx3, txt3, ty3, tyt3, tz3, tzt3, tza, ma, ym, expand,
     out_solution, out_residual,
     send_y, recv_y, send_z, recv_z, send_zs, recv_zs, send_s, recv_s,
     send_a, recv_a, send_az, recv_az, send_pz, recv_pz, send_py, recv_py,
     mats3, kb, rb, wb, slope_one, slope_two, act, tan, back, pred0, qb, lb,
     sy, ry, sz, rz, ss, rs, sa, ra, spz, rpz, spy, rpy) = refs
    me_z, me_y = lax.axis_index("gz"), lax.axis_index("gy")
    core, chip = lax.rem(me_z, 2), lax.div(me_z, 2)
    chunk = s.kxhi * s.rows
    f32 = jnp.float32

    barrier = pltpu.get_barrier_semaphore()
    for k in range(1, s.gy):
        pl.semaphore_signal(barrier, inc=1, device_id={"gy": lax.rem(me_y + k, s.gy)}, device_id_type=MESH)

    def greet(k, carry):
        pl.semaphore_signal(barrier, inc=1, device_id={"gz": lax.rem(me_z + k, s.gz)}, device_id_type=MESH)
        return carry

    lax.fori_loop(1, s.gz, greet, 0)
    pl.semaphore_wait(barrier, s.gy + s.gz - 2)

    hops = sorted(range(1, s.gy), key=lambda k: -min(k, s.gy - k))

    def exchange_gy(src_of, dst, send_sem, recv_sem):
        for k in hops:
            peer = lax.rem(me_y + k, s.gy)
            pltpu.make_async_remote_copy(
                src_of(peer), dst, send_sem, recv_sem, device_id={"gy": peer}, device_id_type=MESH
            ).start()
        pltpu.make_async_copy(src_of(me_y), dst, recv_sem).start()

    def exchange_gz(src_of, dst, send_sem, recv_sem):
        def step(k, carry):
            peer = lax.rem(me_z + k, s.gz)
            pltpu.make_async_remote_copy(
                src_of(peer), dst, send_sem, recv_sem, device_id={"gz": peer}, device_id_type=MESH
            ).start()
            return carry

        lax.fori_loop(1, s.gz, step, 0)
        pltpu.make_async_copy(src_of(me_z), dst, recv_sem).start()

    def wait(ref, sem):
        pltpu.make_async_copy(ref, ref, sem).wait()

    def unit_gy(e):
        exchange_gy(
            lambda p: send_y.at[e, pl.ds(pl.multiple_of(p * chunk, chunk), chunk)],
            recv_y.at[e, pl.ds(pl.multiple_of(me_y * chunk, chunk), chunk)],
            sy.at[e], ry.at[e],
        )

    def wait_gy(e):
        wait(recv_y.at[e], ry.at[e])

    def unit_gz(e):
        if e in SUMS:
            i = SUMS[e]
            exchange_gz(lambda p: send_zs.at[i, p], recv_zs.at[i, me_z], sz.at[e], rz.at[e])
        else:
            exchange_gz(lambda p: send_z.at[e, p], recv_z.at[e, me_z], sz.at[e], rz.at[e])

    def wait_gz(e):
        if e in SUMS:
            wait(recv_zs.at[SUMS[e]], rz.at[e])
        else:
            wait(recv_z.at[e], rz.at[e])

    lane = lax.broadcasted_iota(jnp.int32, (1, 128), 1)
    low_half = (lane < 64).astype(f32)
    high_half = 1.0 - low_half

    both = jnp.concatenate([kappa[...], rhs[...], jnp.zeros((128 - 4 * s.rows, 128), f32)], axis=0)
    spectrum = lax.dot_general(tx[...], both, NT, precision=HIGHEST, preferred_element_type=f32)
    own = jnp.sum(rhs[...] * rhs[...], axis=0, keepdims=True)
    send_a[...] = jnp.zeros_like(send_a)
    for h in range(s.gy):
        send_a[h, 0 : s.kxhi, :] = spectrum[h * s.kxhi : (h + 1) * s.kxhi]
        send_a[h, s.kxhi : s.kxhi + 1, :] = own
    exchange_gy(lambda p: send_a.at[p], recv_a.at[me_y], sa.at[0], ra.at[0])

    for m in range(mats.shape[0]):
        high, low = split(mats[m])
        mats3[m, 0:128, :] = high
        mats3[m, 128:256, :] = low
        mats3[m, 256:384, :] = high
    mix_two, mix_back, read_mat, lift_mat = range(4)

    gain_mix = jnp.zeros((s.modes, 128), f32)
    bias_mix = jnp.zeros((8, 128), f32)
    for t in range(32):
        gain_mix = gain_mix + w1[:, t * 128 : (t + 1) * 128] * gexp[0:1, t * 128 : (t + 1) * 128]
        bias_mix = bias_mix + w1[0:8, t * 128 : (t + 1) * 128] * gexp[1:2, t * 128 : (t + 1) * 128]
    gain_mix = gain_mix + pltpu.roll(gain_mix, 64, 1)
    bias_mix = bias_mix + pltpu.roll(bias_mix, 64, 1)
    is_mean = ((me_z == 0) & (me_y == 0)).astype(f32)
    first_row = (lax.broadcasted_iota(jnp.int32, (8, 128), 0) == 0).astype(f32)
    volume = math.sqrt(float(2 * s.gz) * float(s.rows * s.gy) * float(s.line))
    bias_mix = bias_mix * first_row * (is_mean * volume)

    wait(recv_a, ra.at[0])
    mixed = jnp.zeros((8, 128), f32)
    own = jnp.zeros((1, 128), f32)
    for d in range(s.gy):
        mixed = mixed + jnp.dot(recv_a[d], ma[d], precision=HIGHEST, preferred_element_type=f32)
        own = own + recv_a[d, s.kxhi : s.kxhi + 1, :]
    for c in range(2):
        send_az[c, 0:2, :] = mixed[2 * c : 2 * c + 2]
        send_az[c, 2:3, :] = own
        send_az[c, 3:4, :] = jnp.zeros((1, 128), f32)
    exchange_gz(lambda p: send_az.at[lax.rem(p, 2)], recv_az.at[me_z], sa.at[1], ra.at[1])

    def spread(y, carry):
        for src, dst in ((kappa, kb), (rhs, rb), (weight, wb)):
            near = jnp.broadcast_to(src[pl.ds(y, 1), :], (64, 128))
            far = jnp.broadcast_to(src[pl.ds(s.rows + y, 1), :], (64, 128))
            dst[y] = jnp.concatenate([near, far], axis=0).T
        return carry

    lax.fori_loop(0, s.rows, spread, 0)

    wait(recv_az, ra.at[1])
    arrived = recv_az[...].reshape(4 * s.gz, 128)
    row = lax.broadcasted_iota(jnp.int32, (4 * s.gz, 128), 0)
    norm_zero = total(jnp.where(lax.rem(row, 4) == 2, arrived, 0.0))
    coeffs = jnp.dot(tza[...], arrived, precision=HIGHEST, preferred_element_type=f32)

    def pick(f):
        columns = []
        for j in range(2):
            kept = jnp.zeros((s.kz, 128), f32)
            for z in range(2):
                at = (2 * j + z) * s.kz
                kept = kept + coeffs[at : at + s.kz] * (lane == chip * 4 + z * 2 + f).astype(f32)
            columns.append(jnp.sum(kept, axis=1, keepdims=True))
        return jnp.concatenate(columns, axis=0)

    modes_kappa, modes_rhs = pick(0), pick(1)

    def cells_z(e, values):
        pieces = []
        for j in range(2):
            half = values[j * s.kz : (j + 1) * s.kz]
            pieces += [half * low_half, half * high_half]
        sent = dot(tzt3[...], tall3(jnp.concatenate(pieces, axis=0)))
        send_z[e] = sent.reshape(s.gz, 2, 128)
        unit_gz(e)

    def cells_y(e):
        wait_gz(e)
        send_y[e] = dot(tyt3[...], tall3(recv_z[e].reshape(2 * s.gz, 128)))
        unit_gy(e)

    def cells_x(e, y):
        return dot(txt3[...], tall3(recv_y[e, pl.ds(y, s.kx, stride=s.rows), :]))

    def modes_x(e, y, field):
        send_y[e, pl.ds(y, s.kx, stride=s.rows), :] = dot(tx3[...], tall3(field))

    def modes_sum(e, partial):
        i = SUMS[e]
        send_s[i] = jnp.broadcast_to(partial, (8, 128))
        exchange_gy(lambda p: send_s.at[i], recv_s.at[i, me_y], ss.at[i], rs.at[i])

    def modes_y(e):
        wait_gy(e)
        highs, lows = [], []
        for a in range(s.kxhi):
            for d in range(s.gy):
                at = d * chunk + a * s.rows
                high, low = split(recv_y[e, at : at + s.rows, :])
                highs.append(high)
                lows.append(low)
        sent = dot(ty3[...], jnp.concatenate(highs + highs + lows, axis=0)).reshape(s.gz, 2, 128)
        if e in SUMS:
            i = SUMS[e]
            wait(recv_s.at[i], rs.at[i])
            partial = jnp.zeros((1, 128), f32)
            for d in range(s.gy):
                partial = partial + recv_s[i, d, 0:1, :]
            send_zs[i, :, 0:2, :] = sent
            send_zs[i, :, 2:4, :] = jnp.broadcast_to(partial[None], (s.gz, 2, 128))
        else:
            send_z[e] = sent
        unit_gz(e)

    def modes_z(e):
        wait_gz(e)
        summed = None
        if e in SUMS:
            i = SUMS[e]
            arrived = recv_zs[i, :, 0:2, :].reshape(2 * s.gz, 128)
            summed = total(recv_zs[i, :, 2:3, :].reshape(s.gz, 128))
        else:
            arrived = recv_z[e].reshape(2 * s.gz, 128)
        coeffs = dot(tz3[...], tall3(arrived))
        pieces = []
        for j in range(2):
            at = 2 * j * s.kz
            pieces.append(coeffs[at : at + s.kz] * low_half + coeffs[at + s.kz : at + 2 * s.kz] * high_half)
        values = jnp.concatenate(pieces, axis=0)
        return values + pltpu.roll(values, 64, 1), summed

    def mix_forward(values):
        high, low = split(values)
        low_lanes = lane < 64
        packed = jnp.where(low_lanes, high.astype(f32), low.astype(f32)).astype(jnp.bfloat16)
        mixed = jnp.zeros_like(values)
        for t in range(32):
            mixed = mixed + dot(packed, expand[t]) * w2[:, t * 128 : (t + 1) * 128]
        return mixed + pltpu.roll(mixed, 64, 1)

    def mix_adjoint(values):
        mixed = jnp.zeros((2 * s.modes, 128), f32)
        for t in range(32):
            high, low = split(values * w2[:, t * 128 : (t + 1) * 128])
            packed = jnp.concatenate([high, low], axis=0)
            mixed = mixed + lax.dot_general(packed, expand[t], NT, preferred_element_type=f32)
        return mixed[: s.modes] + mixed[s.modes :]

    def scalar_z(i, coeffs):
        pieces = []
        for j in range(2):
            for z in range(2):
                mask = ((lax.div(lane, 2 * s.rows) == 2 * core + j) & (lax.rem(lax.div(lane, s.rows), 2) == z)).astype(f32)
                pieces.append(coeffs[j * s.kz : (j + 1) * s.kz] * mask)
        sent = dot(tzt3[...], tall3(jnp.concatenate(pieces, axis=0)))
        send_pz[i] = sent.reshape(s.gz, 2, 128)
        exchange_gz(lambda p: send_pz.at[i, p], recv_pz.at[i, me_z], spz.at[i], rpz.at[i])

    def scalar_y(i):
        wait(recv_pz.at[i], rpz.at[i])
        arrived = recv_pz[i].reshape(2 * s.gz, 128)
        for d in range(s.gy):
            send_py[i, d] = jnp.broadcast_to(jnp.sum(arrived * ym[d], axis=0, keepdims=True), (8, 128))
        exchange_gy(lambda p: send_py.at[i, p], recv_py.at[i, me_y], spy.at[i], rpy.at[i])

    def scalar_x(i):
        wait(recv_py.at[i], rpy.at[i])
        rows = jnp.concatenate([recv_py[i, h, 0:1, :] for h in range(s.gy)], axis=0)
        columns = rows.T
        field = jnp.zeros((2 * s.rows, 128), f32)
        for a in range(s.kxhi):
            field = field + jnp.dot(
                columns[a * 2 * s.rows : (a + 1) * 2 * s.rows], txk[a], precision=HIGHEST, preferred_element_type=f32
            )
        return field

    def mat(m, field3):
        return dot(field3, mats3[m])

    def over_rows(body, carry):
        return lax.fori_loop(0, s.rows, body, carry, unroll=UNROLL)

    lift_row, bias_one, bias_two, read_row = vec[0:1, :], vec[1:2, :], vec[2:3, :], vec[3:4, :]
    empty = jnp.zeros((1, 128), f32)

    values = modes_kappa * gain_mix
    cells_z(B0K, jnp.concatenate([values[0:8] + bias_mix, values[8:]], axis=0))
    cells_z(B0R, modes_rhs * gain_mix)
    cells_y(B0K)
    cells_y(B0R)
    wait_gy(B0K)

    def first_point(y, carry):
        pre = cells_x(B0K, y) + lift_row * kb[y] + bias_one
        value, slope = gelu_parts(pre)
        act[y] = value
        slope_one[y] = slope
        modes_x(C0A, y, value)
        return carry

    over_rows(first_point, 0)
    unit_gy(C0A)
    wait_gy(B0R)

    def first_tangent(y, carry):
        value = slope_one[y] * (cells_x(B0R, y) + lift_row * rb[y])
        tan[y] = value
        modes_x(C0T, y, value)
        return carry

    over_rows(first_tangent, 0)
    unit_gy(C0T)
    modes_y(C0A)
    modes_y(C0T)
    values, _ = modes_z(C0A)
    cells_z(D0A, mix_forward(values))
    values, _ = modes_z(C0T)
    cells_z(D0T, mix_forward(values))
    cells_y(D0A)
    cells_y(D0T)
    wait_gy(D0A)

    def second_point(y, carry):
        pre = cells_x(D0A, y) + mat(mix_two, flat3(act[y])) + bias_two
        _, slope = gelu_parts(pre)
        slope_two[y] = slope
        return carry

    over_rows(second_point, 0)
    wait_gy(D0T)

    def second_tangent(y, carry):
        slope = slope_two[y]
        tangent = slope * (cells_x(D0T, y) + mat(mix_two, flat3(tan[y])))
        predicted = mat(read_mat, flat3(tangent))
        pred0[y] = predicted
        weighted = wb[y] * predicted
        value = slope * (read_row * weighted)
        back[y] = value
        modes_x(E0, y, value)
        return carry + jnp.sum(weighted * predicted, axis=0, keepdims=True)

    norms = over_rows(second_tangent, empty)
    modes_sum(E0, norms)
    unit_gy(E0)
    modes_y(E0)
    values, curvature = modes_z(E0)
    curvature = curvature * (1.0 / 64.0) + DAMPING * norm_zero
    step_zero = norm_zero / curvature
    cells_z(F0, mix_adjoint(values))
    cells_y(F0)
    wait_gy(F0)

    def local_rows(y, field3):
        rows = lax.dot_general(mats3[4, 0:16, :], field3[:, 0:128], NT, preferred_element_type=f32)
        rows = rows + lax.dot_general(mats3[4, 128:144, :], field3[:, 0:128], NT, preferred_element_type=f32)
        rows = rows + lax.dot_general(mats3[4, 0:16, :], field3[:, 256:384], NT, preferred_element_type=f32)
        return rows

    def first_back(y, carry):
        value = slope_one[y] * (cells_x(F0, y) + mat(mix_back, flat3(back[y])))
        modes_x(G0, y, value)
        value3 = flat3(value)
        rows = local_rows(y, value3)
        lb[0, pl.ds(y, 1), :] = rows[0:1]
        lb[0, pl.ds(s.rows + y, 1), :] = rows[1:2]
        qb[y] = rb[y] * (1.0 - DAMPING * step_zero) - step_zero * mat(lift_mat, value3)
        return carry

    over_rows(first_back, 0)
    unit_gy(G0)
    modes_y(G0)
    values, _ = modes_z(G0)

    coeffs_zero = jnp.sum(values * gain_mix * low_half, axis=1, keepdims=True)
    image = coeffs_zero + jnp.sum(values * lift_row * low_half, axis=1, keepdims=True) + DAMPING * modes_rhs
    modes_res = modes_rhs - step_zero * image
    cells_z(B1, modes_res * gain_mix - (step_zero * coeffs_zero) * lift_row)
    scalar_z(0, coeffs_zero)
    cells_y(B1)
    scalar_y(0)
    wait_gy(B1)

    def next_tangent(y, carry):
        value = slope_one[y] * (cells_x(B1, y) + lift_row * qb[y])
        tan[y] = value
        modes_x(C1, y, value)
        return carry

    over_rows(next_tangent, 0)
    right = rhs[...]
    applied_zero = scalar_x(0) + lb[0] + DAMPING * right
    residual = right - step_zero * applied_zero
    modes_sum(C1, jnp.sum(residual * residual, axis=0, keepdims=True))
    unit_gy(C1)
    modes_y(C1)
    values, norm_one = modes_z(C1)
    cells_z(D1, mix_forward(values))
    ratio = norm_one / norm_zero
    direction = residual + ratio * right
    cells_y(D1)
    wait_gy(D1)

    def next_second(y, carry):
        slope = slope_two[y]
        tangent = slope * (cells_x(D1, y) + mat(mix_two, flat3(tan[y])))
        predicted = mat(read_mat, flat3(tangent))
        value = slope * (read_row * (wb[y] * predicted))
        back[y] = value
        modes_x(E1, y, value)
        moved = predicted + ratio * pred0[y]
        return carry + jnp.sum(wb[y] * moved * moved, axis=0, keepdims=True)

    norms = over_rows(next_second, empty)
    norms = norms * (1.0 / 64.0) + DAMPING * jnp.sum(direction * direction, axis=0, keepdims=True)
    modes_sum(E1, norms)
    unit_gy(E1)
    modes_y(E1)
    values, curvature = modes_z(E1)
    step_one = norm_one / curvature
    cells_z(F1, mix_adjoint(values))
    cells_y(F1)
    wait_gy(F1)

    def next_back(y, carry):
        value = slope_one[y] * (cells_x(F1, y) + mat(mix_back, flat3(back[y])))
        modes_x(G1, y, value)
        rows = local_rows(y, flat3(value))
        lb[1, pl.ds(y, 1), :] = rows[0:1]
        lb[1, pl.ds(s.rows + y, 1), :] = rows[1:2]
        return carry

    over_rows(next_back, 0)
    unit_gy(G1)
    modes_y(G1)
    values, _ = modes_z(G1)
    scalar_z(1, jnp.sum(values * gain_mix * low_half, axis=1, keepdims=True))
    scalar_y(1)
    applied = scalar_x(1) + lb[1] + DAMPING * residual + ratio * applied_zero
    out_solution[...] = step_zero * right + step_one * direction
    out_residual[...] = residual - step_one * applied

    def sent_gy(ref, sem):
        wait(ref, sem)

    for e in range(UNITS):
        wait(send_y.at[e, pl.ds(0, (s.gy - 1) * chunk)], sy.at[e])
        if e in SUMS:
            wait(send_zs.at[SUMS[e], pl.ds(0, s.gz - 1)], sz.at[e])
        else:
            wait(send_z.at[e, pl.ds(0, s.gz - 1)], sz.at[e])
    for i in range(3):
        wait(recv_s.at[i, pl.ds(0, s.gy - 1)], ss.at[i])
    wait(send_a.at[pl.ds(0, s.gy - 1)], sa.at[0])
    wait(recv_az.at[pl.ds(0, s.gz - 1)], sa.at[1])
    for i in range(2):
        wait(send_pz.at[i, pl.ds(0, s.gz - 1)], spz.at[i])
        wait(send_py.at[i, pl.ds(0, s.gy - 1)], spy.at[i])


def local(
    s,
    log_kappa,
    misfit_weight,
    right_side,
    lift_gain,
    lift_bias,
    spec_one,
    spec_two,
    local_one,
    local_two,
    bias_one,
    bias_two,
    readout,
):
    shape = log_kappa.shape
    rows = lambda x: x.reshape(2 * s.rows, s.line)
    lift_local = jnp.dot(lift_gain, local_one, precision=HIGHEST)
    bias_local = jnp.dot(lift_bias, local_one, precision=HIGHEST)
    vec = jnp.stack([lift_local, bias_local + bias_one, bias_two, readout])
    vec = jnp.concatenate([vec, vec], axis=1)
    vec = jnp.concatenate([vec, jnp.zeros_like(vec)], axis=0)
    gexp = jnp.repeat(jnp.stack([lift_gain, lift_bias]), 64, axis=1)
    gexp = jnp.concatenate([gexp, jnp.zeros((6, 4096), jnp.float32)], axis=0)
    same = np.kron(np.eye(2, dtype=np.float32), np.ones((64, 64), np.float32))
    column = lambda v: jnp.broadcast_to(jnp.concatenate([v, v])[:, None], (128, 128))
    two_rows = jnp.concatenate([same[0:1], same[64:65], jnp.zeros((126, 128), jnp.float32)], axis=0) * vec[0:1]
    mats = jnp.stack(
        [
            jnp.tile(local_two, (2, 2)) * same,
            jnp.tile(local_two.T, (2, 2)) * same,
            column(readout) * same,
            column(lift_local) * same,
            two_rows,
        ]
    )
    operands = [
        rows(log_kappa), rows(misfit_weight), rows(right_side), vec, gexp,
        spec_one.reshape(s.modes, 4096), spec_two.reshape(s.modes, 4096), mats,
    ] + [jnp.asarray(t) for t in tables_of(s)]
    f32, bf16 = jnp.float32, jnp.bfloat16
    vmem = lambda *dims: pltpu.VMEM(dims, f32)
    half = s.kx * s.rows
    cell = (s.rows, 128, 128)
    scratch = [
        vmem(UNITS, half, 128), vmem(UNITS, half, 128),
        vmem(UNITS, s.gz, 2, 128), vmem(UNITS, s.gz, 2, 128),
        vmem(3, s.gz, 4, 128), vmem(3, s.gz, 4, 128),
        vmem(3, 8, 128), vmem(3, s.gy, 8, 128),
        vmem(s.gy, 8, 128), vmem(s.gy, 8, 128),
        vmem(2, 4, 128), vmem(s.gz, 4, 128),
        vmem(2, s.gz, 2, 128), vmem(2, s.gz, 2, 128),
        vmem(2, s.gy, 8, 128), vmem(2, s.gy, 8, 128),
        pltpu.VMEM((5, 384, 128), bf16),
    ] + [vmem(*cell) for _ in range(10)] + [vmem(2, 2 * s.rows, 128)]
    counts = [UNITS] * 4 + [3, 3, 2, 2, 2, 2, 2, 2]
    scratch += [pltpu.SemaphoreType.DMA((n,)) for n in counts]
    results = pl.pallas_call(
        functools.partial(kernel, s),
        out_shape=[jax.ShapeDtypeStruct((2 * s.rows, s.line), f32)] * 2,
        in_specs=[pl.BlockSpec(memory_space=pltpu.VMEM)] * len(operands),
        out_specs=[pl.BlockSpec(memory_space=pltpu.VMEM)] * 2,
        scratch_shapes=scratch,
        compiler_params=pltpu.CompilerParams(
            collective_id=0, has_side_effects=True, vmem_limit_bytes=60 * 1024 * 1024
        ),
        name="two_steps",
    )(*operands)
    return tuple(x.reshape(shape) for x in results)


def solution(mesh, kx=KX, ky=KY, kz=KZ, rows=16, line=128):
    s = Sizes(mesh.shape["gz"], mesh.shape["gy"], rows, line, kx, ky, kz)
    field = P("gz", "gy", None)
    weights = P("gz", "gy", None, None)
    return jax.shard_map(
        functools.partial(local, s),
        mesh=mesh,
        in_specs=(field, field, field, P(), P(), weights, weights, P(), P(), P(), P(), P()),
        out_specs=(field, field),
        check_vma=False,
    )
```

time: 1020 us -> 280 us (0.27)
  blocking collectives: 631 us -> 0 us
  Pallas kernels: 0 us -> 270 us
  matrix products: 125 us -> 0.27 us
  waiting for transfers between devices: 105 us -> 0 us
  starting transfers between devices: 91 us -> 0 us
  local copies, waits for them, and re-layouts: 52.1 us -> 7.18 us
    all_to_all x24 -> x0, blocking collectives: 348 us -> none  [the longest x6 91.6 us: to_modes(): lax.all_to_all(spectra, 'gz', split_axis=1, concat_axis=0, tiled=True)]
    psum x3 -> x0, blocking collectives: 283 us -> none  [the longest x2 189 us: residual_sum(): return lax.psum(jnp.sum(values * values), ('gz', 'gy'))]
    pallas_call x0 -> x1, Pallas kernels: none -> 270 us  [local(): pl.pallas_call(functools.partial(kernel, s), out_shape=[jax.ShapeDtypeStr...]
    dot_general x81 -> x0, matrix products: 125 us -> none  [the longest x10 30.6 us: to_modes(): jnp.einsum('czyx,irx->zyric', grid_field, table_x, precision=HIGHEST)]
    all_to_all x16 -> x0, waiting for transfers between devices: 105 us -> none  [the longest x4 29.9 us: to_cells(): lax.all_to_all(row_data, 'gy', split_axis=1, concat_axis=2, tiled=True)]
    all_to_all x16 -> x0, starting transfers between devices: 91 us -> none  [the longest x4 29.5 us: to_modes(): lax.all_to_all(spectra, 'gz', split_axis=1, concat_axis=0, tiled=True)]
    reshape x82 -> x1, local copies, waits for them, and re-layouts: 41.5 us -> 0.1 us  [local(): gexp = jnp.repeat(jnp.stack([lift_gain, lift_bias]), 64, axis=1)]
  transfers between devices with their start and end apart: 16 -> 0, of which waited for: 15 -> 0; matrix products, arithmetic and copies ran while one was open for 6% -> 0% of each run, Pallas kernels for 0% -> 0%
where the time goes in v1:
time: 280 us; the launch traced here: 279 us
  Pallas kernels  270 us (96%)
  local copies, waits for them, and re-layouts  7.18 us (3%)
    pallas_call x1, Pallas kernels, local(): pl.pallas_call(functools.partial(kernel, s), out_shape=[jax.ShapeDtypeStr...  270 us

profile of v1, /device:TPU:1, one launch (start us, length us, event | category | flops | bytes accessed | tf_op | source)
XLA Modules:
  0.0 279.2 jit_solution(5318647193978040524)
XLA Ops:
  0.6 0.0 copy-start
  0.6 0.0 copy-start.3
  0.7 0.9 copy.29
  1.6 0.0 copy-done.3
  1.6 1.0 broadcast_multiply_fusion
  2.6 0.1 stack.48
  2.7 0.1 stack.49
  2.9 0.6 copy-done.9
  3.5 0.1 pad_maximum_fusion.1
  3.6 0.1 copy-done.2
  3.7 0.1 bitcast_dynamic-update-slice_fusion.1
  3.8 0.0 copy-done
  3.8 0.6 copy-done.7
  4.3 0.1 fusion.3
  4.5 0.1 pad_maximum_fusion.2
  4.6 0.1 bitcast_dynamic-update-slice_fusion
  4.7 0.6 copy-done.6
  5.2 0.0 copy-done.8
  5.2 0.1 fusion.1
  5.4 0.7 copy-done.10
  6.0 0.1 maximum_maximum_fusion
  6.1 0.0 copy-done.4
  6.1 0.0 copy-start.1
  6.1 0.6 concatenate.30.refs_3_
  6.8 0.1 broadcast_in_dim.8
  6.9 0.1 reshape.95
  7.0 0.7 concatenate.31.refs_4_
  7.6 0.0 copy-done.1
  7.6 269.6 %two_steps.1 = (f32[32,128]{1,0:T(8,128)}, f32[32,128]{1,0:T(8,128)}) custom-call(f32[32,128]{1,0:T(8,128)} %bitcast.38, f32[32,128]{1,0:T(8,128)} %bitcast.39, f32[32,128]{1,0:T(8,128)} %bitcast.40, f32[8,128]{1,0:T(8,128)} %concatenate.30.refs_3_, f32[8,4096]{1,0:T(8,128)} %concatenate.31.refs_4_, f32[64,4096]{1,0:T(8,128)} %bitcast.35, ...), custom_call_target="tpu_custom_call" | custom-call | tf_op jit(solution)/shard_map/two_steps/pallas_call | solution.py:615
  277.2 0.0 copy-start.5
  277.2 1.3 copy.36
  278.6 0.6 copy.37
  (13 shorter events, 0.0 us)
Async XLA Ops:
  0.6 3.1 %copy-start = (f32[64,64]{1,0:T(8,128)S(1)}, f32[64,64]{1,0:T(8,128)}, u32[]{:S(2)}) copy-start(f32[64,64]{1,0:T(8,128)} %param.34) | copy-start | bytes 49156
  0.6 0.9 copy-start.3
  2.8 0.7 copy-start.9
  2.8 0.9 copy-start.2
  3.7 0.7 copy-start.7
  4.6 0.7 copy-start.6
  4.6 0.7 copy-start.8
  4.6 1.6 copy-start.4
  5.4 0.7 copy-start.10
  6.1 1.5 copy-start.1
  277.2 1.3 copy-start.5

commit v2 on v1

--- a/solution.py
+++ b/solution.py
@@ -20,7 +20,7 @@
 UNITS = 15
 B0K, B0R, C0A, C0T, D0A, D0T, E0, F0, G0, B1, C1, D1, E1, F1, G1 = range(UNITS)
 SUMS = {E0: 0, C1: 1, E1: 2}
-UNROLL = 2
+PIECES = 4
 
 
 def basis_table(modes, length):
@@ -50,6 +50,11 @@
         self.kx, self.ky, self.kz = kx, ky, kz
         self.kxhi = kx // gy
         self.modes = ky * self.kxhi // gz * kz
+        self.nx = 4 if gz >= 32 else 1
+        self.ny = gz // 2 // self.nx
+        self.deep = rows // PIECES
+        self.block = kx * self.deep
+        self.part = self.kxhi * self.deep
 
 
 def tables_of(s):
@@ -57,9 +62,10 @@
     order = np.arange(s.kx).reshape(s.kxhi, s.gy).T.reshape(-1)
     tx = bx[order]
     eye = np.eye(s.kxhi, dtype=np.float32)
-    ty = np.einsum("kY,ab->kabY", by, eye).reshape(s.ky * s.kxhi, s.kxhi * s.rows * s.gy)
     byd = by.reshape(s.ky, s.gy, s.rows)
-    tyt = np.einsum("kdy,ab->dayKb".replace("K", "k"), byd, eye).reshape(s.gy * s.kxhi * s.rows, s.ky * s.kxhi)
+    byp = by.reshape(s.ky, s.gy, PIECES, s.deep)
+    ty = np.einsum("kdpy,ab->pkadby", byp, eye).reshape(PIECES, s.ky * s.kxhi, s.block)
+    tyt = np.einsum("kdpy,ab->pdbyka", byp, eye).reshape(PIECES * s.block, s.ky * s.kxhi)
     bzg = bz.reshape(s.kz, s.gz, 2)
     two = np.eye(2, dtype=np.float32)
     tz = np.einsum("kgz,ij->izkgj", bzg, two).reshape(4 * s.kz, 2 * s.gz)
@@ -80,7 +86,7 @@
         bx.reshape(s.kxhi, s.gy, s.line),
         wide(tx),
         wide(np.ascontiguousarray(tx.T)),
-        wide(ty),
+        np.stack([wide(t) for t in ty]),
         wide(tyt),
         wide(tz),
         wide(np.ascontiguousarray(tz.T)),
@@ -88,6 +94,7 @@
         full,
         ym,
         expand.astype(ml_dtypes.bfloat16),
+        np.concatenate([np.eye(64, dtype=np.float32)] * 2, axis=1),
     ]
 
 
@@ -121,30 +128,55 @@
 
 
 def kernel(s, *refs):
-    (kappa, weight, rhs, vec, gexp, w1, w2, mats,
-     tx, txk, tx3, txt3, ty3, tyt3, tz3, tzt3, tza, ma, ym, expand,
+    (kappa, weight, rhs, gain_in, bias_in, b1_in, b2_in, read_in, l1_in, l2_in, tx, txk, tx3, txt3, tz3, tzt3, twice,
+     w1_in, w2_in, ty3_in, tyt3_in, tza_in, ma_in, ym_in, expand_in,
      out_solution, out_residual,
      send_y, recv_y, send_z, recv_z, send_zs, recv_zs, send_s, recv_s,
      send_a, recv_a, send_az, recv_az, send_pz, recv_pz, send_py, recv_py,
-     mats3, kb, rb, wb, slope_one, slope_two, act, tan, back, pred0, qb, lb,
-     sy, ry, sz, rz, ss, rs, sa, ra, spz, rpz, spy, rpy) = refs
+     mats3, kb, rb, wb, slope_one, slope_two, act, tan, back, pred0, qb, lb, vecs,
+     w1, w2, ty3, tyt3, tza, ma, ym, expand,
+     sy, ry, sz, rz, ss, rs, sa, ra, spz, rpz, spy, rpy, loads) = refs
     me_z, me_y = lax.axis_index("gz"), lax.axis_index("gy")
     core, chip = lax.rem(me_z, 2), lax.div(me_z, 2)
-    chunk = s.kxhi * s.rows
+    at_y, at_x = lax.div(chip, s.nx), lax.rem(chip, s.nx)
     f32 = jnp.float32
 
+    brought = {}
+    for i, (src, dst) in enumerate(
+        ((ma_in, ma), (expand_in, expand), (w1_in, w1), (tza_in, tza), (tyt3_in, tyt3), (ty3_in, ty3), (w2_in, w2), (ym_in, ym))
+    ):
+        brought[id(dst)] = pltpu.make_async_copy(src, dst, loads.at[i])
+        brought[id(dst)].start()
+
+    def ready(dst):
+        brought[id(dst)].wait()
+
+    ring_x = sorted(range(s.nx), key=lambda k: -min(k, s.nx - k))
+
+    def peers_gz(visit):
+        def at(dy, dx, dc):
+            y, x = lax.rem(at_y + dy, s.ny), lax.rem(at_x + dx, s.nx)
+            visit((y * s.nx + x) * 2 + lax.rem(core + dc, 2))
+
+        def step(i, carry):
+            dy = s.ny // 2 + lax.div(i + 1, 2) * (1 - 2 * lax.rem(i, 2))
+            for dx in ring_x:
+                for dc in range(2):
+                    at(dy, dx, dc)
+            return carry
+
+        lax.fori_loop(0, s.ny - 1, step, 0)
+        for dx in ring_x:
+            for dc in range(2):
+                if dx or dc:
+                    at(0, dx, dc)
+
+    hops = sorted(range(1, s.gy), key=lambda k: -min(k, s.gy - k))
     barrier = pltpu.get_barrier_semaphore()
-    for k in range(1, s.gy):
+    for k in hops:
         pl.semaphore_signal(barrier, inc=1, device_id={"gy": lax.rem(me_y + k, s.gy)}, device_id_type=MESH)
 
-    def greet(k, carry):
-        pl.semaphore_signal(barrier, inc=1, device_id={"gz": lax.rem(me_z + k, s.gz)}, device_id_type=MESH)
-        return carry
-
-    lax.fori_loop(1, s.gz, greet, 0)
-    pl.semaphore_wait(barrier, s.gy + s.gz - 2)
-
-    hops = sorted(range(1, s.gy), key=lambda k: -min(k, s.gy - k))
+    peers_gz(lambda p: pl.semaphore_signal(barrier, inc=1, device_id={"gz": p}, device_id_type=MESH))
 
     def exchange_gy(src_of, dst, send_sem, recv_sem):
         for k in hops:
@@ -155,28 +187,28 @@
         pltpu.make_async_copy(src_of(me_y), dst, recv_sem).start()
 
     def exchange_gz(src_of, dst, send_sem, recv_sem):
-        def step(k, carry):
-            peer = lax.rem(me_z + k, s.gz)
-            pltpu.make_async_remote_copy(
-                src_of(peer), dst, send_sem, recv_sem, device_id={"gz": peer}, device_id_type=MESH
+        peers_gz(
+            lambda p: pltpu.make_async_remote_copy(
+                src_of(p), dst, send_sem, recv_sem, device_id={"gz": p}, device_id_type=MESH
             ).start()
-            return carry
-
-        lax.fori_loop(1, s.gz, step, 0)
+        )
         pltpu.make_async_copy(src_of(me_z), dst, recv_sem).start()
 
     def wait(ref, sem):
         pltpu.make_async_copy(ref, ref, sem).wait()
 
-    def unit_gy(e):
+    def piece(p):
+        return slice(p * s.block, (p + 1) * s.block)
+
+    def piece_gy(e, p):
         exchange_gy(
-            lambda p: send_y.at[e, pl.ds(pl.multiple_of(p * chunk, chunk), chunk)],
-            recv_y.at[e, pl.ds(pl.multiple_of(me_y * chunk, chunk), chunk)],
-            sy.at[e], ry.at[e],
+            lambda d: send_y.at[e, pl.ds(pl.multiple_of(p * s.block + d * s.part, s.part), s.part)],
+            recv_y.at[e, pl.ds(pl.multiple_of(p * s.block + me_y * s.part, s.part), s.part)],
+            sy.at[e], ry.at[e, p],
         )
 
-    def wait_gy(e):
-        wait(recv_y.at[e], ry.at[e])
+    def wait_gy(e, p):
+        wait(recv_y.at[e, pl.ds(p * s.block, s.block)], ry.at[e, p])
 
     def unit_gz(e):
         if e in SUMS:
@@ -202,10 +234,27 @@
     for h in range(s.gy):
         send_a[h, 0 : s.kxhi, :] = spectrum[h * s.kxhi : (h + 1) * s.kxhi]
         send_a[h, s.kxhi : s.kxhi + 1, :] = own
+    vecs[...] = jnp.zeros_like(vecs)
+    for i, ref in enumerate((gain_in, bias_in, b1_in, b2_in, read_in)):
+        vecs[i : i + 1, :] = ref[...]
+    exact = functools.partial(jnp.dot, precision=HIGHEST, preferred_element_type=f32)
+    doubled = exact(vecs[...], twice[...])
+    lifted = exact(exact(vecs[...], l1_in[...]), twice[...])
+    gain_row, read_row, bias_two = doubled[0:1], doubled[4:5], doubled[3:4]
+    lift_row, bias_one = lifted[0:1], lifted[1:2] + doubled[2:3]
+    same = lax.div(lax.broadcasted_iota(jnp.int32, (128, 128), 0), 64) == lax.div(
+        lax.broadcasted_iota(jnp.int32, (128, 128), 1), 64
+    )
+    only = lambda x: jnp.where(same, x, 0.0)
+    column = lambda x: only(jnp.broadcast_to(x, (128, 128)).T)
+    local_two = only(jnp.concatenate([exact(l2_in[...], twice[...])] * 2, axis=0))
+    row = lax.broadcasted_iota(jnp.int32, (128, 128), 0)
+    two_rows = jnp.where((row == 0) & (lane < 64) | (row == 1) & (lane >= 64), jnp.broadcast_to(lift_row, (128, 128)), 0.0)
+    pl.semaphore_wait(barrier, s.gy + s.gz - 2)
     exchange_gy(lambda p: send_a.at[p], recv_a.at[me_y], sa.at[0], ra.at[0])
 
-    for m in range(mats.shape[0]):
-        high, low = split(mats[m])
+    for m, table in enumerate((local_two, local_two.T, column(read_row), column(lift_row), two_rows)):
+        high, low = split(table)
         mats3[m, 0:128, :] = high
         mats3[m, 128:256, :] = low
         mats3[m, 256:384, :] = high
@@ -213,9 +262,14 @@
 
     gain_mix = jnp.zeros((s.modes, 128), f32)
     bias_mix = jnp.zeros((8, 128), f32)
+    high, low = split(doubled)
+    packed = jnp.where(lane < 64, high.astype(f32), low.astype(f32)).astype(jnp.bfloat16)
+    ready(expand)
+    ready(w1)
     for t in range(32):
-        gain_mix = gain_mix + w1[:, t * 128 : (t + 1) * 128] * gexp[0:1, t * 128 : (t + 1) * 128]
-        bias_mix = bias_mix + w1[0:8, t * 128 : (t + 1) * 128] * gexp[1:2, t * 128 : (t + 1) * 128]
+        spread_rows = dot(packed, expand[t])
+        gain_mix = gain_mix + w1[:, t * 128 : (t + 1) * 128] * spread_rows[0:1]
+        bias_mix = bias_mix + w1[0:8, t * 128 : (t + 1) * 128] * spread_rows[1:2]
     gain_mix = gain_mix + pltpu.roll(gain_mix, 64, 1)
     bias_mix = bias_mix + pltpu.roll(bias_mix, 64, 1)
     is_mean = ((me_z == 0) & (me_y == 0)).astype(f32)
@@ -223,6 +277,7 @@
     volume = math.sqrt(float(2 * s.gz) * float(s.rows * s.gy) * float(s.line))
     bias_mix = bias_mix * first_row * (is_mean * volume)
 
+    ready(ma)
     wait(recv_a, ra.at[0])
     mixed = jnp.zeros((8, 128), f32)
     own = jnp.zeros((1, 128), f32)
@@ -235,15 +290,17 @@
         send_az[c, 3:4, :] = jnp.zeros((1, 128), f32)
     exchange_gz(lambda p: send_az.at[lax.rem(p, 2)], recv_az.at[me_z], sa.at[1], ra.at[1])
 
-    def spread(y, carry):
+    def spread(p, carry):
         for src, dst in ((kappa, kb), (rhs, rb), (weight, wb)):
-            near = jnp.broadcast_to(src[pl.ds(y, 1), :], (64, 128))
-            far = jnp.broadcast_to(src[pl.ds(s.rows + y, 1), :], (64, 128))
-            dst[y] = jnp.concatenate([near, far], axis=0).T
+            for y in range(s.deep):
+                near = jnp.broadcast_to(src[pl.ds(p * s.deep + y, 1), :], (64, 128))
+                far = jnp.broadcast_to(src[pl.ds(s.rows + p * s.deep + y, 1), :], (64, 128))
+                dst[p, :, y * 128 : (y + 1) * 128] = jnp.concatenate([near, far], axis=0).T
         return carry
 
-    lax.fori_loop(0, s.rows, spread, 0)
-
+    lax.fori_loop(0, PIECES, spread, 0)
+
+    ready(tza)
     wait(recv_az, ra.at[1])
     arrived = recv_az[...].reshape(4 * s.gz, 128)
     row = lax.broadcasted_iota(jnp.int32, (4 * s.gz, 128), 0)
@@ -273,14 +330,22 @@
 
     def cells_y(e):
         wait_gz(e)
-        send_y[e] = dot(tyt3[...], tall3(recv_z[e].reshape(2 * s.gz, 128)))
-        unit_gy(e)
-
-    def cells_x(e, y):
-        return dot(txt3[...], tall3(recv_y[e, pl.ds(y, s.kx, stride=s.rows), :]))
-
-    def modes_x(e, y, field):
-        send_y[e, pl.ds(y, s.kx, stride=s.rows), :] = dot(tx3[...], tall3(field))
+        values = tall3(recv_z[e].reshape(2 * s.gz, 128))
+        for p in range(PIECES):
+            send_y[e, piece(p), :] = dot(tyt3[piece(p), :], values)
+            piece_gy(e, p)
+
+    def cells_x(e, p):
+        wait_gy(e, p)
+        rows = [recv_y[e, pl.ds(p * s.block + y, s.kx, stride=s.deep), :] for y in range(s.deep)]
+        return dot(txt3[...], tall3(jnp.concatenate(rows, axis=1)))
+
+    def modes_x(e, p, parts):
+        high, low = parts
+        sent = dot(tx3[...], jnp.concatenate([high, high, low], axis=0))
+        for y in range(s.deep):
+            send_y[e, pl.ds(p * s.block + y, s.kx, stride=s.deep), :] = sent[:, y * 128 : (y + 1) * 128]
+        piece_gy(e, p)
 
     def modes_sum(e, partial):
         i = SUMS[e]
@@ -288,15 +353,11 @@
         exchange_gy(lambda p: send_s.at[i], recv_s.at[i, me_y], ss.at[i], rs.at[i])
 
     def modes_y(e):
-        wait_gy(e)
-        highs, lows = [], []
-        for a in range(s.kxhi):
-            for d in range(s.gy):
-                at = d * chunk + a * s.rows
-                high, low = split(recv_y[e, at : at + s.rows, :])
-                highs.append(high)
-                lows.append(low)
-        sent = dot(ty3[...], jnp.concatenate(highs + highs + lows, axis=0)).reshape(s.gz, 2, 128)
+        sent = jnp.zeros((2 * s.gz, 128), f32)
+        for p in range(PIECES):
+            wait_gy(e, p)
+            sent = sent + dot(ty3[p], tall3(recv_y[e, piece(p), :]))
+        sent = sent.reshape(s.gz, 2, 128)
         if e in SUMS:
             i = SUMS[e]
             wait(recv_s.at[i], rs.at[i])
@@ -371,101 +432,86 @@
             )
         return field
 
-    def mat(m, field3):
-        return dot(field3, mats3[m])
-
-    def over_rows(body, carry):
-        return lax.fori_loop(0, s.rows, body, carry, unroll=UNROLL)
-
-    lift_row, bias_one, bias_two, read_row = vec[0:1, :], vec[1:2, :], vec[2:3, :], vec[3:4, :]
+    def lines(x):
+        return jnp.concatenate([x[:, y * 128 : (y + 1) * 128] for y in range(s.deep)], axis=0)
+
+    def across(x):
+        return jnp.concatenate([x[y * 128 : (y + 1) * 128] for y in range(s.deep)], axis=1)
+
+    def mat(m, parts):
+        high, low = lines(parts[0]), lines(parts[1])
+        return across(dot(jnp.concatenate([high, high, low], axis=1), mats3[m]))
+
+    def fold(x):
+        x = jnp.sum(x, axis=0, keepdims=True)
+        return sum(x[:, y * 128 : (y + 1) * 128] for y in range(s.deep))
+
+    def local_rows(i, p, parts):
+        high, low = lines(parts[0]), lines(parts[1])
+        rows = lax.dot_general(mats3[4, 0:16, :], high, NT, preferred_element_type=f32)
+        rows = rows + lax.dot_general(mats3[4, 128:144, :], high, NT, preferred_element_type=f32)
+        rows = rows + lax.dot_general(mats3[4, 0:16, :], low, NT, preferred_element_type=f32)
+        for y in range(s.deep):
+            lb[i, p * s.deep + y : p * s.deep + y + 1, :] = rows[0:1, y * 128 : (y + 1) * 128]
+            at = s.rows + p * s.deep + y
+            lb[i, at : at + 1, :] = rows[1:2, y * 128 : (y + 1) * 128]
+
+    wide_row = lambda x: jnp.concatenate([x] * s.deep, axis=1)
+    lift_wide, one_wide, two_wide, read_wide = map(wide_row, (lift_row, bias_one, bias_two, read_row))
     empty = jnp.zeros((1, 128), f32)
 
     values = modes_kappa * gain_mix
     cells_z(B0K, jnp.concatenate([values[0:8] + bias_mix, values[8:]], axis=0))
     cells_z(B0R, modes_rhs * gain_mix)
+    ready(tyt3)
     cells_y(B0K)
     cells_y(B0R)
-    wait_gy(B0K)
-
-    def first_point(y, carry):
-        pre = cells_x(B0K, y) + lift_row * kb[y] + bias_one
-        value, slope = gelu_parts(pre)
-        act[y] = value
-        slope_one[y] = slope
-        modes_x(C0A, y, value)
-        return carry
-
-    over_rows(first_point, 0)
-    unit_gy(C0A)
-    wait_gy(B0R)
-
-    def first_tangent(y, carry):
-        value = slope_one[y] * (cells_x(B0R, y) + lift_row * rb[y])
-        tan[y] = value
-        modes_x(C0T, y, value)
-        return carry
-
-    over_rows(first_tangent, 0)
-    unit_gy(C0T)
+    for p in range(PIECES):
+        value, slope = gelu_parts(cells_x(B0K, p) + lift_wide * kb[p] + one_wide)
+        act[p] = value
+        slope_one[p] = slope
+        modes_x(C0A, p, split(value))
+    for p in range(PIECES):
+        value = slope_one[p] * (cells_x(B0R, p) + lift_wide * rb[p])
+        tan[p] = value
+        modes_x(C0T, p, split(value))
+    ready(ty3)
     modes_y(C0A)
     modes_y(C0T)
+    ready(w2)
     values, _ = modes_z(C0A)
     cells_z(D0A, mix_forward(values))
     values, _ = modes_z(C0T)
     cells_z(D0T, mix_forward(values))
     cells_y(D0A)
     cells_y(D0T)
-    wait_gy(D0A)
-
-    def second_point(y, carry):
-        pre = cells_x(D0A, y) + mat(mix_two, flat3(act[y])) + bias_two
-        _, slope = gelu_parts(pre)
-        slope_two[y] = slope
-        return carry
-
-    over_rows(second_point, 0)
-    wait_gy(D0T)
-
-    def second_tangent(y, carry):
-        slope = slope_two[y]
-        tangent = slope * (cells_x(D0T, y) + mat(mix_two, flat3(tan[y])))
-        predicted = mat(read_mat, flat3(tangent))
-        pred0[y] = predicted
-        weighted = wb[y] * predicted
-        value = slope * (read_row * weighted)
-        back[y] = value
-        modes_x(E0, y, value)
-        return carry + jnp.sum(weighted * predicted, axis=0, keepdims=True)
-
-    norms = over_rows(second_tangent, empty)
+    for p in range(PIECES):
+        _, slope = gelu_parts(cells_x(D0A, p) + mat(mix_two, split(act[p])) + two_wide)
+        slope_two[p] = slope
+    norms = empty
+    for p in range(PIECES):
+        slope = slope_two[p]
+        tangent = slope * (cells_x(D0T, p) + mat(mix_two, split(tan[p])))
+        predicted = mat(read_mat, split(tangent))
+        pred0[p] = predicted
+        weighted = wb[p] * predicted
+        value = slope * (read_wide * weighted)
+        back[p] = value
+        modes_x(E0, p, split(value))
+        norms = norms + fold(weighted * predicted)
     modes_sum(E0, norms)
-    unit_gy(E0)
     modes_y(E0)
     values, curvature = modes_z(E0)
     curvature = curvature * (1.0 / 64.0) + DAMPING * norm_zero
     step_zero = norm_zero / curvature
     cells_z(F0, mix_adjoint(values))
     cells_y(F0)
-    wait_gy(F0)
-
-    def local_rows(y, field3):
-        rows = lax.dot_general(mats3[4, 0:16, :], field3[:, 0:128], NT, preferred_element_type=f32)
-        rows = rows + lax.dot_general(mats3[4, 128:144, :], field3[:, 0:128], NT, preferred_element_type=f32)
-        rows = rows + lax.dot_general(mats3[4, 0:16, :], field3[:, 256:384], NT, preferred_element_type=f32)
-        return rows
-
-    def first_back(y, carry):
-        value = slope_one[y] * (cells_x(F0, y) + mat(mix_back, flat3(back[y])))
-        modes_x(G0, y, value)
-        value3 = flat3(value)
-        rows = local_rows(y, value3)
-        lb[0, pl.ds(y, 1), :] = rows[0:1]
-        lb[0, pl.ds(s.rows + y, 1), :] = rows[1:2]
-        qb[y] = rb[y] * (1.0 - DAMPING * step_zero) - step_zero * mat(lift_mat, value3)
-        return carry
-
-    over_rows(first_back, 0)
-    unit_gy(G0)
+    for p in range(PIECES):
+        value = slope_one[p] * (cells_x(F0, p) + mat(mix_back, split(back[p])))
+        parts = split(value)
+        modes_x(G0, p, parts)
+        local_rows(0, p, parts)
+        qb[p] = rb[p] * (1.0 - DAMPING * step_zero) - step_zero * mat(lift_mat, parts)
     modes_y(G0)
     values, _ = modes_z(G0)
 
@@ -475,60 +521,44 @@
     cells_z(B1, modes_res * gain_mix - (step_zero * coeffs_zero) * lift_row)
     scalar_z(0, coeffs_zero)
     cells_y(B1)
+    ready(ym)
     scalar_y(0)
-    wait_gy(B1)
-
-    def next_tangent(y, carry):
-        value = slope_one[y] * (cells_x(B1, y) + lift_row * qb[y])
-        tan[y] = value
-        modes_x(C1, y, value)
-        return carry
-
-    over_rows(next_tangent, 0)
+    for p in range(PIECES):
+        value = slope_one[p] * (cells_x(B1, p) + lift_wide * qb[p])
+        tan[p] = value
+        modes_x(C1, p, split(value))
     right = rhs[...]
     applied_zero = scalar_x(0) + lb[0] + DAMPING * right
     residual = right - step_zero * applied_zero
     modes_sum(C1, jnp.sum(residual * residual, axis=0, keepdims=True))
-    unit_gy(C1)
     modes_y(C1)
     values, norm_one = modes_z(C1)
     cells_z(D1, mix_forward(values))
     ratio = norm_one / norm_zero
     direction = residual + ratio * right
     cells_y(D1)
-    wait_gy(D1)
-
-    def next_second(y, carry):
-        slope = slope_two[y]
-        tangent = slope * (cells_x(D1, y) + mat(mix_two, flat3(tan[y])))
-        predicted = mat(read_mat, flat3(tangent))
-        value = slope * (read_row * (wb[y] * predicted))
-        back[y] = value
-        modes_x(E1, y, value)
-        moved = predicted + ratio * pred0[y]
-        return carry + jnp.sum(wb[y] * moved * moved, axis=0, keepdims=True)
-
-    norms = over_rows(next_second, empty)
+    norms = empty
+    for p in range(PIECES):
+        slope = slope_two[p]
+        tangent = slope * (cells_x(D1, p) + mat(mix_two, split(tan[p])))
+        predicted = mat(read_mat, split(tangent))
+        value = slope * (read_wide * (wb[p] * predicted))
+        back[p] = value
+        modes_x(E1, p, split(value))
+        moved = predicted + ratio * pred0[p]
+        norms = norms + fold(wb[p] * moved * moved)
     norms = norms * (1.0 / 64.0) + DAMPING * jnp.sum(direction * direction, axis=0, keepdims=True)
     modes_sum(E1, norms)
-    unit_gy(E1)
     modes_y(E1)
     values, curvature = modes_z(E1)
     step_one = norm_one / curvature
     cells_z(F1, mix_adjoint(values))
     cells_y(F1)
-    wait_gy(F1)
-
-    def next_back(y, carry):
-        value = slope_one[y] * (cells_x(F1, y) + mat(mix_back, flat3(back[y])))
-        modes_x(G1, y, value)
-        rows = local_rows(y, flat3(value))
-        lb[1, pl.ds(y, 1), :] = rows[0:1]
-        lb[1, pl.ds(s.rows + y, 1), :] = rows[1:2]
-        return carry
-
-    over_rows(next_back, 0)
-    unit_gy(G1)
+    for p in range(PIECES):
+        value = slope_one[p] * (cells_x(F1, p) + mat(mix_back, split(back[p])))
+        parts = split(value)
+        modes_x(G1, p, parts)
+        local_rows(1, p, parts)
     modes_y(G1)
     values, _ = modes_z(G1)
     scalar_z(1, jnp.sum(values * gain_mix * low_half, axis=1, keepdims=True))
@@ -537,11 +567,8 @@
     out_solution[...] = step_zero * right + step_one * direction
     out_residual[...] = residual - step_one * applied
 
-    def sent_gy(ref, sem):
-        wait(ref, sem)
-
     for e in range(UNITS):
-        wait(send_y.at[e, pl.ds(0, (s.gy - 1) * chunk)], sy.at[e])
+        wait(send_y.at[e, pl.ds(0, PIECES * (s.gy - 1) * s.part)], sy.at[e])
         if e in SUMS:
             wait(send_zs.at[SUMS[e], pl.ds(0, s.gz - 1)], sz.at[e])
         else:
@@ -572,33 +599,19 @@
 ):
     shape = log_kappa.shape
     rows = lambda x: x.reshape(2 * s.rows, s.line)
-    lift_local = jnp.dot(lift_gain, local_one, precision=HIGHEST)
-    bias_local = jnp.dot(lift_bias, local_one, precision=HIGHEST)
-    vec = jnp.stack([lift_local, bias_local + bias_one, bias_two, readout])
-    vec = jnp.concatenate([vec, vec], axis=1)
-    vec = jnp.concatenate([vec, jnp.zeros_like(vec)], axis=0)
-    gexp = jnp.repeat(jnp.stack([lift_gain, lift_bias]), 64, axis=1)
-    gexp = jnp.concatenate([gexp, jnp.zeros((6, 4096), jnp.float32)], axis=0)
-    same = np.kron(np.eye(2, dtype=np.float32), np.ones((64, 64), np.float32))
-    column = lambda v: jnp.broadcast_to(jnp.concatenate([v, v])[:, None], (128, 128))
-    two_rows = jnp.concatenate([same[0:1], same[64:65], jnp.zeros((126, 128), jnp.float32)], axis=0) * vec[0:1]
-    mats = jnp.stack(
-        [
-            jnp.tile(local_two, (2, 2)) * same,
-            jnp.tile(local_two.T, (2, 2)) * same,
-            column(readout) * same,
-            column(lift_local) * same,
-            two_rows,
-        ]
-    )
-    operands = [
-        rows(log_kappa), rows(misfit_weight), rows(right_side), vec, gexp,
-        spec_one.reshape(s.modes, 4096), spec_two.reshape(s.modes, 4096), mats,
-    ] + [jnp.asarray(t) for t in tables_of(s)]
+    row = lambda x: x.reshape(1, 64)
+    tables = [jnp.asarray(t) for t in tables_of(s)]
+    tx, txk, tx3, txt3, ty3, tyt3, tz3, tzt3, tza, ma, ym, expand, twice = tables
+    near = [
+        rows(log_kappa), rows(misfit_weight), rows(right_side),
+        row(lift_gain), row(lift_bias), row(bias_one), row(bias_two), row(readout),
+        local_one, local_two, tx, txk, tx3, txt3, tz3, tzt3, twice,
+    ]
+    far = [spec_one.reshape(s.modes, 4096), spec_two.reshape(s.modes, 4096), ty3, tyt3, tza, ma, ym, expand]
     f32, bf16 = jnp.float32, jnp.bfloat16
     vmem = lambda *dims: pltpu.VMEM(dims, f32)
     half = s.kx * s.rows
-    cell = (s.rows, 128, 128)
+    cell = (PIECES, 128, 128 * s.deep)
     scratch = [
         vmem(UNITS, half, 128), vmem(UNITS, half, 128),
         vmem(UNITS, s.gz, 2, 128), vmem(UNITS, s.gz, 2, 128),
@@ -609,20 +622,21 @@
         vmem(2, s.gz, 2, 128), vmem(2, s.gz, 2, 128),
         vmem(2, s.gy, 8, 128), vmem(2, s.gy, 8, 128),
         pltpu.VMEM((5, 384, 128), bf16),
-    ] + [vmem(*cell) for _ in range(10)] + [vmem(2, 2 * s.rows, 128)]
-    counts = [UNITS] * 4 + [3, 3, 2, 2, 2, 2, 2, 2]
-    scratch += [pltpu.SemaphoreType.DMA((n,)) for n in counts]
+    ] + [vmem(*cell) for _ in range(10)] + [vmem(2, 2 * s.rows, 128), vmem(8, 64)]
+    scratch += [pltpu.VMEM(x.shape, x.dtype) for x in far]
+    counts = [(UNITS,), (UNITS, PIECES), (UNITS,), (UNITS,), (3,), (3,), (2,), (2,), (2,), (2,), (2,), (2,), (len(far),)]
+    scratch += [pltpu.SemaphoreType.DMA(n) for n in counts]
     results = pl.pallas_call(
         functools.partial(kernel, s),
         out_shape=[jax.ShapeDtypeStruct((2 * s.rows, s.line), f32)] * 2,
-        in_specs=[pl.BlockSpec(memory_space=pltpu.VMEM)] * len(operands),
+        in_specs=[pl.BlockSpec(memory_space=pltpu.VMEM)] * len(near) + [pl.BlockSpec(memory_space=pl.ANY)] * len(far),
         out_specs=[pl.BlockSpec(memory_space=pltpu.VMEM)] * 2,
         scratch_shapes=scratch,
         compiler_params=pltpu.CompilerParams(
             collective_id=0, has_side_effects=True, vmem_limit_bytes=60 * 1024 * 1024
         ),
         name="two_steps",
-    )(*operands)
+    )(*near, *far)
     return tuple(x.reshape(shape) for x in results)
 
 

time: 280 us -> 226 us (0.81)
  Pallas kernels: 270 us -> 223 us
  local copies, waits for them, and re-layouts: 7.18 us -> 1.94 us
    pallas_call x1, Pallas kernels: 270 us -> 223 us  [local(): pl.pallas_call(functools.partial(kernel, s), out_shape=[jax.ShapeDtypeStr...]
where the time goes in v2:
time: 226 us
  Pallas kernels  223 us (99%)
    pallas_call x1, Pallas kernels, local(): pl.pallas_call(functools.partial(kernel, s), out_shape=[jax.ShapeDtypeStr...  223 us

profile of v2, /device:TPU:1, one launch (start us, length us, event | category | flops | bytes accessed | tf_op | source)
XLA Modules:
  0.0 225.9 jit_solution(8820633266489612509)
XLA Ops:
  0.6 223.3 %two_steps.1 = (f32[32,128]{1,0:T(8,128)}, f32[32,128]{1,0:T(8,128)}) custom-call(f32[32,128]{1,0:T(8,128)} %bitcast.14, f32[32,128]{1,0:T(8,128)} %bitcast.15, f32[32,128]{1,0:T(8,128)} %bitcast.16, f32[1,64]{1,0:T(1,128)} %bitcast.19, f32[1,64]{1,0:T(1,128)} %bitcast.20, f32[1,64]{1,0:T(1,128)} %bitcast.21, f32[1,64]{1,0:T(1,128)} %bitcast.22, ...), custom_call_target="tpu_custom_call" | custom-call | tf_op jit(solution)/shard_map/two_steps/pallas_call | solution.py:629
  223.9 0.0 copy-start
  224.0 1.3 copy.29
  225.3 0.0 copy-done
  225.3 0.6 copy.30
Async XLA Ops:
  223.9 1.3 copy-start

commit v3 on v2

--- a/solution.py
+++ b/solution.py
@@ -21,6 +21,7 @@
 B0K, B0R, C0A, C0T, D0A, D0T, E0, F0, G0, B1, C1, D1, E1, F1, G1 = range(UNITS)
 SUMS = {E0: 0, C1: 1, E1: 2}
 PIECES = 4
+NX = 4
 
 
 def basis_table(modes, length):
@@ -48,28 +49,23 @@
     def __init__(self, gz, gy, rows, line, kx, ky, kz):
         self.gz, self.gy, self.rows, self.line = gz, gy, rows, line
         self.kx, self.ky, self.kz = kx, ky, kz
-        self.kxhi = kx // gy
-        self.modes = ky * self.kxhi // gz * kz
-        self.nx = 4 if gz >= 32 else 1
-        self.ny = gz // 2 // self.nx
+        self.modes = 2 * kz
+        self.ny = gz // 2 // NX
+        self.light = 2 * self.ny
+        self.heavy = NX * gy
         self.deep = rows // PIECES
         self.block = kx * self.deep
-        self.part = self.kxhi * self.deep
 
 
 def tables_of(s):
     bx, by, bz = basis_table(s.kx, s.line), basis_table(s.ky, s.rows * s.gy), basis_table(s.kz, 2 * s.gz)
-    order = np.arange(s.kx).reshape(s.kxhi, s.gy).T.reshape(-1)
-    tx = bx[order]
-    eye = np.eye(s.kxhi, dtype=np.float32)
+    bx = bx[np.arange(s.kx).reshape(NX, s.gy).T.reshape(-1)]
     byd = by.reshape(s.ky, s.gy, s.rows)
-    byp = by.reshape(s.ky, s.gy, PIECES, s.deep)
-    ty = np.einsum("kdpy,ab->pkadby", byp, eye).reshape(PIECES, s.ky * s.kxhi, s.block)
-    tyt = np.einsum("kdpy,ab->pdbyka", byp, eye).reshape(PIECES * s.block, s.ky * s.kxhi)
-    bzg = bz.reshape(s.kz, s.gz, 2)
+    ty = by.reshape(s.ky, s.gy, PIECES, s.deep).transpose(0, 2, 1, 3).reshape(s.ky, PIECES, s.gy * s.deep)
+    bzg = bz.reshape(s.kz, s.ny, NX, 2, 2)
     two = np.eye(2, dtype=np.float32)
-    tz = np.einsum("kgz,ij->izkgj", bzg, two).reshape(4 * s.kz, 2 * s.gz)
-    tza = np.einsum("kgz,ij->izkgj", bzg, np.eye(2, 4, dtype=np.float32)).reshape(4 * s.kz, 4 * s.gz)
+    tz = np.einsum("kyxaz,ij->izkyajx", bzg, two).reshape(4 * s.kz, 8 * s.light)
+    tza = np.einsum("kyxaz,r->zkyaxr", bzg, np.eye(1, 2, dtype=np.float32)[0]).reshape(2 * s.kz, 8 * s.light)
     ma = np.zeros((s.gy, 2, 2, s.rows, s.ky, 2, 2), np.float32)
     for f in range(2):
         for z in range(2):
@@ -77,17 +73,19 @@
     ma = ma.reshape(s.gy, 4 * s.rows, 4 * s.ky)
     full = np.zeros((s.gy, 128, 128), np.float32)
     full[:, : 4 * s.rows, : 4 * s.ky] = ma
-    ym = np.broadcast_to(byd.transpose(1, 0, 2)[:, :, None, None, None, :], (s.gy, s.ky, s.kxhi, s.kxhi, 2, s.rows))
-    ym = np.ascontiguousarray(ym).reshape(s.gy, s.ky * s.kxhi, s.kxhi * 2 * s.rows)
-    lanes = np.arange(128)
-    expand = (np.arange(128)[None, :, None] % 64 == 2 * np.arange(32)[:, None, None] + lanes[None, None, :] // 64)
+    ym = np.broadcast_to(byd.transpose(1, 0, 2)[:, :, None, None, None, :], (s.gy, s.ky, NX, NX, 2, s.rows))
+    ym = np.ascontiguousarray(ym).reshape(s.gy, s.ky * NX, NX * 2 * s.rows)
+    txs = np.zeros((s.kx, 2, s.line), np.float32)
+    txs[:, 0] = bx
+    lanes = np.arange(256)
+    expand = (np.arange(128)[None, :, None] % 64 == 4 * np.arange(16)[:, None, None] + lanes[None, None, :] // 64)
     return [
-        tx,
-        bx.reshape(s.kxhi, s.gy, s.line),
-        wide(tx),
-        wide(np.ascontiguousarray(tx.T)),
-        np.stack([wide(t) for t in ty]),
-        wide(tyt),
+        bx,
+        txs.reshape(2 * s.kx, s.line),
+        wide(bx),
+        wide(np.ascontiguousarray(bx.T)),
+        np.stack([wide(ty[:, p]) for p in range(PIECES)]),
+        wide(np.ascontiguousarray(ty.reshape(s.ky, -1).T)),
         wide(tz),
         wide(np.ascontiguousarray(tz.T)),
         tza,
@@ -130,20 +128,21 @@
 def kernel(s, *refs):
     (kappa, weight, rhs, gain_in, bias_in, b1_in, b2_in, read_in, l1_in, l2_in, tx, txk, tx3, txt3, tz3, tzt3, twice,
      w1_in, w2_in, ty3_in, tyt3_in, tza_in, ma_in, ym_in, expand_in,
-     out_solution, out_residual,
+     out,
      send_y, recv_y, send_z, recv_z, send_zs, recv_zs, send_s, recv_s,
      send_a, recv_a, send_az, recv_az, send_pz, recv_pz, send_py, recv_py,
-     mats3, kb, rb, wb, slope_one, slope_two, act, tan, back, pred0, qb, lb, vecs,
+     mats3, kb, rb, wb, slope_one, slope_two, act, tan, back, pred0, qb, lb, vecs, plane, gain_own, gain_new,
      w1, w2, ty3, tyt3, tza, ma, ym, expand,
-     sy, ry, sz, rz, ss, rs, sa, ra, spz, rpz, spy, rpy, loads) = refs
+     sy, ry, sz, rz, ss, rs, sa, ra, spz, rpz, spy, rpy, sw, rw, loads) = refs
     me_z, me_y = lax.axis_index("gz"), lax.axis_index("gy")
     core, chip = lax.rem(me_z, 2), lax.div(me_z, 2)
-    at_y, at_x = lax.div(chip, s.nx), lax.rem(chip, s.nx)
+    at_y, at_x = lax.div(chip, NX), lax.rem(chip, NX)
+    me_light, me_heavy = at_y * 2 + core, me_y * NX + at_x
     f32 = jnp.float32
 
     brought = {}
     for i, (src, dst) in enumerate(
-        ((ma_in, ma), (expand_in, expand), (w1_in, w1), (tza_in, tza), (tyt3_in, tyt3), (ty3_in, ty3), (w2_in, w2), (ym_in, ym))
+        ((ma_in, ma), (expand_in, expand), (w1_in, w1), (tza_in, tza), (tyt3_in, tyt3), (ty3_in, ty3), (ym_in, ym))
     ):
         brought[id(dst)] = pltpu.make_async_copy(src, dst, loads.at[i])
         brought[id(dst)].start()
@@ -151,48 +150,72 @@
     def ready(dst):
         brought[id(dst)].wait()
 
-    ring_x = sorted(range(s.nx), key=lambda k: -min(k, s.nx - k))
-
-    def peers_gz(visit):
-        def at(dy, dx, dc):
-            y, x = lax.rem(at_y + dy, s.ny), lax.rem(at_x + dx, s.nx)
-            visit((y * s.nx + x) * 2 + lax.rem(core + dc, 2))
-
-        def step(i, carry):
-            dy = s.ny // 2 + lax.div(i + 1, 2) * (1 - 2 * lax.rem(i, 2))
-            for dx in ring_x:
-                for dc in range(2):
-                    at(dy, dx, dc)
-            return carry
-
-        lax.fori_loop(0, s.ny - 1, step, 0)
-        for dx in ring_x:
-            for dc in range(2):
-                if dx or dc:
-                    at(0, dx, dc)
-
-    hops = sorted(range(1, s.gy), key=lambda k: -min(k, s.gy - k))
+    def place(y, x, c):
+        return (y * NX + x) * 2 + c
+
+    def far_first(*rings):
+        steps = [()]
+        for n in rings:
+            steps = [step + (k,) for step in steps for k in range(n)]
+        far = lambda step: -sum(min(k, n - k) for k, n in zip(step, rings))
+        return sorted((step for step in steps if any(step)), key=far)
+
+    heavy_steps, light_steps = far_first(s.gy, NX), far_first(s.ny, 2)
+
+    def peers_heavy(visit):
+        for dz, dx in heavy_steps:
+            z, x = lax.rem(me_y + dz, s.gy), lax.rem(at_x + dx, NX)
+            visit(z * NX + x, {"gz": place(at_y, x, core), "gy": z})
+
+    def peers_light(visit):
+        for dy, dc in light_steps:
+            y, c = lax.rem(at_y + dy, s.ny), lax.rem(core + dc, 2)
+            visit(y * 2 + c, {"gz": place(y, at_x, c)})
+
+    new_core, new_slot = lax.div(at_x, 2), lax.rem(at_x, 2)
+    movers = [(2 * core + j, place(at_y, 2 * core + j, new_core)) for j in range(2)]
+
     barrier = pltpu.get_barrier_semaphore()
-    for k in hops:
-        pl.semaphore_signal(barrier, inc=1, device_id={"gy": lax.rem(me_y + k, s.gy)}, device_id_type=MESH)
-
-    peers_gz(lambda p: pl.semaphore_signal(barrier, inc=1, device_id={"gz": p}, device_id_type=MESH))
-
-    def exchange_gy(src_of, dst, send_sem, recv_sem):
-        for k in hops:
-            peer = lax.rem(me_y + k, s.gy)
-            pltpu.make_async_remote_copy(
-                src_of(peer), dst, send_sem, recv_sem, device_id={"gy": peer}, device_id_type=MESH
-            ).start()
-        pltpu.make_async_copy(src_of(me_y), dst, recv_sem).start()
-
-    def exchange_gz(src_of, dst, send_sem, recv_sem):
-        peers_gz(
-            lambda p: pltpu.make_async_remote_copy(
-                src_of(p), dst, send_sem, recv_sem, device_id={"gz": p}, device_id_type=MESH
+    greet = lambda _, device: pl.semaphore_signal(barrier, inc=1, device_id=device, device_id_type=MESH)
+    peers_heavy(greet)
+    peers_light(greet)
+    for dx in range(1, NX):
+        greet(None, {"gz": place(at_y, lax.rem(at_x + dx, NX), 1 - core)})
+    greeted = len(heavy_steps) + len(light_steps) + NX - 1
+
+    def exchange_heavy(src_of, dst, send_sem, recv_sem):
+        peers_heavy(
+            lambda n, device: pltpu.make_async_remote_copy(
+                src_of(n), dst, send_sem, recv_sem, device_id=device, device_id_type=MESH
             ).start()
         )
-        pltpu.make_async_copy(src_of(me_z), dst, recv_sem).start()
+        pltpu.make_async_copy(src_of(me_heavy), dst, recv_sem).start()
+
+    def exchange_light(src_of, dst, send_sem, recv_sem):
+        peers_light(
+            lambda n, device: pltpu.make_async_remote_copy(
+                src_of(n), dst, send_sem, recv_sem, device_id=device, device_id_type=MESH
+            ).start()
+        )
+        pltpu.make_async_copy(src_of(me_light), dst, recv_sem).start()
+
+    def move(src_of, dst, send_sem, recv_sem):
+        for j, (x, target) in enumerate(movers):
+            @pl.when(target != me_z)
+            def _():
+                pltpu.make_async_remote_copy(
+                    src_of(j), dst.at[new_slot], send_sem, recv_sem, device_id={"gz": target}, device_id_type=MESH
+                ).start()
+
+            @pl.when(target == me_z)
+            def _():
+                pltpu.make_async_copy(src_of(j), dst.at[new_slot], recv_sem).start()
+
+    def left(src_of, send_sem):
+        for j, (x, target) in enumerate(movers):
+            @pl.when(target != me_z)
+            def _():
+                wait(src_of(j), send_sem)
 
     def wait(ref, sem):
         pltpu.make_async_copy(ref, ref, sem).wait()
@@ -201,21 +224,21 @@
         return slice(p * s.block, (p + 1) * s.block)
 
     def piece_gy(e, p):
-        exchange_gy(
-            lambda d: send_y.at[e, pl.ds(pl.multiple_of(p * s.block + d * s.part, s.part), s.part)],
-            recv_y.at[e, pl.ds(pl.multiple_of(p * s.block + me_y * s.part, s.part), s.part)],
-            sy.at[e], ry.at[e, p],
-        )
+        rows = lambda n: pl.ds(pl.multiple_of(p * s.block + n * s.deep, s.deep), s.deep)
+        exchange_heavy(lambda n: send_y.at[e, rows(n)], recv_y.at[e, rows(me_heavy)], sy.at[e], ry.at[e, p])
 
     def wait_gy(e, p):
         wait(recv_y.at[e, pl.ds(p * s.block, s.block)], ry.at[e, p])
+
+    def eight(n):
+        return pl.ds(pl.multiple_of(n * 8, 8), 8)
 
     def unit_gz(e):
         if e in SUMS:
             i = SUMS[e]
-            exchange_gz(lambda p: send_zs.at[i, p], recv_zs.at[i, me_z], sz.at[e], rz.at[e])
+            exchange_light(lambda n: send_zs.at[i, n], recv_zs.at[i, me_light], sz.at[e], rz.at[e])
         else:
-            exchange_gz(lambda p: send_z.at[e, p], recv_z.at[e, me_z], sz.at[e], rz.at[e])
+            exchange_light(lambda n: send_z.at[e, eight(n)], recv_z.at[e, eight(me_light)], sz.at[e], rz.at[e])
 
     def wait_gz(e):
         if e in SUMS:
@@ -230,10 +253,9 @@
     both = jnp.concatenate([kappa[...], rhs[...], jnp.zeros((128 - 4 * s.rows, 128), f32)], axis=0)
     spectrum = lax.dot_general(tx[...], both, NT, precision=HIGHEST, preferred_element_type=f32)
     own = jnp.sum(rhs[...] * rhs[...], axis=0, keepdims=True)
-    send_a[...] = jnp.zeros_like(send_a)
-    for h in range(s.gy):
-        send_a[h, 0 : s.kxhi, :] = spectrum[h * s.kxhi : (h + 1) * s.kxhi]
-        send_a[h, s.kxhi : s.kxhi + 1, :] = own
+    for k in range(s.kx):
+        send_a[k, 0:1, :] = spectrum[k : k + 1]
+        send_a[k, 1:2, :] = own
     vecs[...] = jnp.zeros_like(vecs)
     for i, ref in enumerate((gain_in, bias_in, b1_in, b2_in, read_in)):
         vecs[i : i + 1, :] = ref[...]
@@ -250,8 +272,8 @@
     local_two = only(jnp.concatenate([exact(l2_in[...], twice[...])] * 2, axis=0))
     row = lax.broadcasted_iota(jnp.int32, (128, 128), 0)
     two_rows = jnp.where((row == 0) & (lane < 64) | (row == 1) & (lane >= 64), jnp.broadcast_to(lift_row, (128, 128)), 0.0)
-    pl.semaphore_wait(barrier, s.gy + s.gz - 2)
-    exchange_gy(lambda p: send_a.at[p], recv_a.at[me_y], sa.at[0], ra.at[0])
+    pl.semaphore_wait(barrier, greeted)
+    exchange_heavy(lambda n: send_a.at[n], recv_a.at[me_heavy], sa.at[0], ra.at[0])
 
     for m, table in enumerate((local_two, local_two.T, column(read_row), column(lift_row), two_rows)):
         high, low = split(table)
@@ -266,11 +288,16 @@
     packed = jnp.where(lane < 64, high.astype(f32), low.astype(f32)).astype(jnp.bfloat16)
     ready(expand)
     ready(w1)
-    for t in range(32):
+    for t in range(16):
         spread_rows = dot(packed, expand[t])
-        gain_mix = gain_mix + w1[:, t * 128 : (t + 1) * 128] * spread_rows[0:1]
-        bias_mix = bias_mix + w1[0:8, t * 128 : (t + 1) * 128] * spread_rows[1:2]
-    gain_mix = gain_mix + pltpu.roll(gain_mix, 64, 1)
+        for u in range(2):
+            at = (2 * t + u) * 128
+            part = spread_rows[:, u * 128 : (u + 1) * 128]
+            gain_mix = gain_mix + w1[:, at : at + 128] * part[0:1]
+            bias_mix = bias_mix + w1[0:8, at : at + 128] * part[1:2]
+    gain_own[...] = (gain_mix + pltpu.roll(gain_mix, 64, 1)).reshape(2, s.kz, 128)
+    move(lambda j: gain_own.at[j], gain_new, sw.at[0], rw.at[0])
+    move(lambda j: w2_in.at[j], w2, sw.at[1], rw.at[1])
     bias_mix = bias_mix + pltpu.roll(bias_mix, 64, 1)
     is_mean = ((me_z == 0) & (me_y == 0)).astype(f32)
     first_row = (lax.broadcasted_iota(jnp.int32, (8, 128), 0) == 0).astype(f32)
@@ -280,15 +307,14 @@
     ready(ma)
     wait(recv_a, ra.at[0])
     mixed = jnp.zeros((8, 128), f32)
-    own = jnp.zeros((1, 128), f32)
+    own = jnp.zeros((8, 128), f32)
     for d in range(s.gy):
-        mixed = mixed + jnp.dot(recv_a[d], ma[d], precision=HIGHEST, preferred_element_type=f32)
-        own = own + recv_a[d, s.kxhi : s.kxhi + 1, :]
-    for c in range(2):
-        send_az[c, 0:2, :] = mixed[2 * c : 2 * c + 2]
-        send_az[c, 2:3, :] = own
-        send_az[c, 3:4, :] = jnp.zeros((1, 128), f32)
-    exchange_gz(lambda p: send_az.at[lax.rem(p, 2)], recv_az.at[me_z], sa.at[1], ra.at[1])
+        rows = recv_a[d * NX : (d + 1) * NX].reshape(8, 128)
+        mixed = mixed + jnp.dot(rows, ma[d], precision=HIGHEST, preferred_element_type=f32)
+        own = own + rows
+    odd = (lax.rem(lax.broadcasted_iota(jnp.int32, (8, 128), 0), 2) == 1)
+    send_az[...] = jnp.where(odd, own, mixed)
+    exchange_light(lambda n: send_az, recv_az.at[eight(me_light)], sa.at[1], ra.at[1])
 
     def spread(p, carry):
         for src, dst in ((kappa, kb), (rhs, rb), (weight, wb)):
@@ -302,9 +328,9 @@
 
     ready(tza)
     wait(recv_az, ra.at[1])
-    arrived = recv_az[...].reshape(4 * s.gz, 128)
-    row = lax.broadcasted_iota(jnp.int32, (4 * s.gz, 128), 0)
-    norm_zero = total(jnp.where(lax.rem(row, 4) == 2, arrived, 0.0))
+    arrived = recv_az[...]
+    row = lax.broadcasted_iota(jnp.int32, arrived.shape, 0)
+    norm_zero = total(jnp.where(lax.rem(row, 2) == 1, arrived, 0.0))
     coeffs = jnp.dot(tza[...], arrived, precision=HIGHEST, preferred_element_type=f32)
 
     def pick(f):
@@ -312,27 +338,36 @@
         for j in range(2):
             kept = jnp.zeros((s.kz, 128), f32)
             for z in range(2):
-                at = (2 * j + z) * s.kz
-                kept = kept + coeffs[at : at + s.kz] * (lane == chip * 4 + z * 2 + f).astype(f32)
+                at = (4 * at_y + 2 * core + j) * 4 + z * 2 + f
+                kept = kept + coeffs[z * s.kz : (z + 1) * s.kz] * (lane == at).astype(f32)
             columns.append(jnp.sum(kept, axis=1, keepdims=True))
         return jnp.concatenate(columns, axis=0)
 
     modes_kappa, modes_rhs = pick(0), pick(1)
+    wait(gain_new, rw.at[0])
+    gain_mix = gain_new[...].reshape(s.modes, 128)
 
     def cells_z(e, values):
         pieces = []
         for j in range(2):
             half = values[j * s.kz : (j + 1) * s.kz]
             pieces += [half * low_half, half * high_half]
-        sent = dot(tzt3[...], tall3(jnp.concatenate(pieces, axis=0)))
-        send_z[e] = sent.reshape(s.gz, 2, 128)
+        send_z[e] = dot(tzt3[...], tall3(jnp.concatenate(pieces, axis=0)))
         unit_gz(e)
+
+    def groups(ref, *at):
+        return jnp.concatenate([ref[(*at, pl.ds(x, s.ky, stride=NX), slice(None))] for x in range(NX)], axis=1)
 
     def cells_y(e):
         wait_gz(e)
-        values = tall3(recv_z[e].reshape(2 * s.gz, 128))
+        values = tall3(groups(recv_z, e))
+        half = s.gy * s.deep
         for p in range(PIECES):
-            send_y[e, piece(p), :] = dot(tyt3[piece(p), :], values)
+            sent = dot(tyt3[p * half : (p + 1) * half, :], values)
+            for d in range(s.gy):
+                for x in range(NX):
+                    at = p * s.block + (d * NX + x) * s.deep
+                    send_y[e, at : at + s.deep, :] = sent[d * s.deep : (d + 1) * s.deep, x * 128 : (x + 1) * 128]
             piece_gy(e, p)
 
     def cells_x(e, p):
@@ -349,25 +384,26 @@
 
     def modes_sum(e, partial):
         i = SUMS[e]
-        send_s[i] = jnp.broadcast_to(partial, (8, 128))
-        exchange_gy(lambda p: send_s.at[i], recv_s.at[i, me_y], ss.at[i], rs.at[i])
+        send_s[i] = jnp.broadcast_to(partial, (2, 128))
+        exchange_heavy(lambda n: send_s.at[i], recv_s.at[i, me_heavy], ss.at[i], rs.at[i])
 
     def modes_y(e):
-        sent = jnp.zeros((2 * s.gz, 128), f32)
+        sent = jnp.zeros((s.ky, NX * 128), f32)
         for p in range(PIECES):
             wait_gy(e, p)
-            sent = sent + dot(ty3[p], tall3(recv_y[e, piece(p), :]))
-        sent = sent.reshape(s.gz, 2, 128)
+            field = []
+            for x in range(NX):
+                at = [p * s.block + (d * NX + x) * s.deep for d in range(s.gy)]
+                field.append(jnp.concatenate([recv_y[e, a : a + s.deep, :] for a in at], axis=0))
+            sent = sent + dot(ty3[p], tall3(jnp.concatenate(field, axis=1)))
+        for x in range(NX):
+            send_z[e, pl.ds(x, s.ky, stride=NX), :] = sent[:, x * 128 : (x + 1) * 128]
         if e in SUMS:
             i = SUMS[e]
             wait(recv_s.at[i], rs.at[i])
-            partial = jnp.zeros((1, 128), f32)
-            for d in range(s.gy):
-                partial = partial + recv_s[i, d, 0:1, :]
-            send_zs[i, :, 0:2, :] = sent
-            send_zs[i, :, 2:4, :] = jnp.broadcast_to(partial[None], (s.gz, 2, 128))
-        else:
-            send_z[e] = sent
+            partial = jnp.sum(recv_s[i].reshape(2 * s.heavy, 128), axis=0, keepdims=True) * 0.5
+            send_zs[i, :, 0:8, :] = send_z[e].reshape(s.light, 8, 128)
+            send_zs[i, :, 8:16, :] = jnp.broadcast_to(partial[None], (s.light, 8, 128))
         unit_gz(e)
 
     def modes_z(e):
@@ -375,10 +411,10 @@
         summed = None
         if e in SUMS:
             i = SUMS[e]
-            arrived = recv_zs[i, :, 0:2, :].reshape(2 * s.gz, 128)
-            summed = total(recv_zs[i, :, 2:3, :].reshape(s.gz, 128))
+            arrived = recv_zs[i, :, 0:8, :].reshape(8 * s.light, 128)
+            summed = total(recv_zs[i, :, 8:9, :].reshape(s.light, 128))
         else:
-            arrived = recv_z[e].reshape(2 * s.gz, 128)
+            arrived = recv_z[e]
         coeffs = dot(tz3[...], tall3(arrived))
         pieces = []
         for j in range(2):
@@ -392,14 +428,17 @@
         low_lanes = lane < 64
         packed = jnp.where(low_lanes, high.astype(f32), low.astype(f32)).astype(jnp.bfloat16)
         mixed = jnp.zeros_like(values)
-        for t in range(32):
-            mixed = mixed + dot(packed, expand[t]) * w2[:, t * 128 : (t + 1) * 128]
+        mixed = jnp.zeros((s.modes, 256), f32)
+        for t in range(16):
+            mixed = mixed + dot(packed, expand[t]) * w2[:, :, t * 256 : (t + 1) * 256].reshape(s.modes, 256)
+        mixed = mixed[:, :128] + mixed[:, 128:]
         return mixed + pltpu.roll(mixed, 64, 1)
 
     def mix_adjoint(values):
         mixed = jnp.zeros((2 * s.modes, 128), f32)
-        for t in range(32):
-            high, low = split(values * w2[:, t * 128 : (t + 1) * 128])
+        values = jnp.concatenate([values, values], axis=1)
+        for t in range(16):
+            high, low = split(values * w2[:, :, t * 256 : (t + 1) * 256].reshape(s.modes, 256))
             packed = jnp.concatenate([high, low], axis=0)
             mixed = mixed + lax.dot_general(packed, expand[t], NT, preferred_element_type=f32)
         return mixed[: s.modes] + mixed[s.modes :]
@@ -408,29 +447,28 @@
         pieces = []
         for j in range(2):
             for z in range(2):
-                mask = ((lax.div(lane, 2 * s.rows) == 2 * core + j) & (lax.rem(lax.div(lane, s.rows), 2) == z)).astype(f32)
+                mask = (lax.rem(lax.div(lane, s.rows), 2) == z).astype(f32)
                 pieces.append(coeffs[j * s.kz : (j + 1) * s.kz] * mask)
         sent = dot(tzt3[...], tall3(jnp.concatenate(pieces, axis=0)))
-        send_pz[i] = sent.reshape(s.gz, 2, 128)
-        exchange_gz(lambda p: send_pz.at[i, p], recv_pz.at[i, me_z], spz.at[i], rpz.at[i])
+        row = lax.broadcasted_iota(jnp.int32, sent.shape, 0)
+        send_pz[i] = jnp.where(lax.rem(row, NX) == lax.div(lane, 2 * s.rows), sent, 0.0)
+        exchange_light(lambda n: send_pz.at[i, eight(n)], recv_pz.at[i, eight(me_light)], spz.at[i], rpz.at[i])
 
     def scalar_y(i):
         wait(recv_pz.at[i], rpz.at[i])
-        arrived = recv_pz[i].reshape(2 * s.gz, 128)
+        arrived = recv_pz[i]
         for d in range(s.gy):
-            send_py[i, d] = jnp.broadcast_to(jnp.sum(arrived * ym[d], axis=0, keepdims=True), (8, 128))
-        exchange_gy(lambda p: send_py.at[i, p], recv_py.at[i, me_y], spy.at[i], rpy.at[i])
+            summed = jnp.sum(arrived * ym[d], axis=0, keepdims=True)
+            send_py[i, d] = jnp.broadcast_to(summed, (2, 128))
+        exchange_heavy(
+            lambda n: send_py.at[i, lax.div(n, NX)], recv_py.at[i, me_heavy], spy.at[i], rpy.at[i]
+        )
 
     def scalar_x(i):
         wait(recv_py.at[i], rpy.at[i])
-        rows = jnp.concatenate([recv_py[i, h, 0:1, :] for h in range(s.gy)], axis=0)
-        columns = rows.T
-        field = jnp.zeros((2 * s.rows, 128), f32)
-        for a in range(s.kxhi):
-            field = field + jnp.dot(
-                columns[a * 2 * s.rows : (a + 1) * 2 * s.rows], txk[a], precision=HIGHEST, preferred_element_type=f32
-            )
-        return field
+        columns = recv_py[i].reshape(2 * s.heavy, 128).T
+        plane[...] = jnp.dot(columns, txk[...], precision=HIGHEST, preferred_element_type=f32)
+        return plane[pl.ds(pl.multiple_of(at_x * 2 * s.rows, 2 * s.rows), 2 * s.rows), :]
 
     def lines(x):
         return jnp.concatenate([x[:, y * 128 : (y + 1) * 128] for y in range(s.deep)], axis=0)
@@ -478,7 +516,7 @@
     ready(ty3)
     modes_y(C0A)
     modes_y(C0T)
-    ready(w2)
+    wait(w2, rw.at[1])
     values, _ = modes_z(C0A)
     cells_z(D0A, mix_forward(values))
     values, _ = modes_z(C0T)
@@ -564,22 +602,24 @@
     scalar_z(1, jnp.sum(values * gain_mix * low_half, axis=1, keepdims=True))
     scalar_y(1)
     applied = scalar_x(1) + lb[1] + DAMPING * residual + ratio * applied_zero
-    out_solution[...] = step_zero * right + step_one * direction
-    out_residual[...] = residual - step_one * applied
+    out[0] = step_zero * right + step_one * direction
+    out[1] = residual - step_one * applied
 
     for e in range(UNITS):
-        wait(send_y.at[e, pl.ds(0, PIECES * (s.gy - 1) * s.part)], sy.at[e])
+        wait(send_y.at[e, pl.ds(0, s.rows * (s.heavy - 1))], sy.at[e])
         if e in SUMS:
-            wait(send_zs.at[SUMS[e], pl.ds(0, s.gz - 1)], sz.at[e])
+            wait(send_zs.at[SUMS[e], pl.ds(0, s.light - 1)], sz.at[e])
         else:
-            wait(send_z.at[e, pl.ds(0, s.gz - 1)], sz.at[e])
+            wait(send_z.at[e, pl.ds(0, 8 * (s.light - 1))], sz.at[e])
     for i in range(3):
-        wait(recv_s.at[i, pl.ds(0, s.gy - 1)], ss.at[i])
-    wait(send_a.at[pl.ds(0, s.gy - 1)], sa.at[0])
-    wait(recv_az.at[pl.ds(0, s.gz - 1)], sa.at[1])
+        wait(recv_s.at[i, pl.ds(0, s.heavy - 1)], ss.at[i])
+    wait(send_a.at[pl.ds(0, s.heavy - 1)], sa.at[0])
+    wait(recv_az.at[pl.ds(0, 8 * (s.light - 1))], sa.at[1])
     for i in range(2):
-        wait(send_pz.at[i, pl.ds(0, s.gz - 1)], spz.at[i])
-        wait(send_py.at[i, pl.ds(0, s.gy - 1)], spy.at[i])
+        wait(send_pz.at[i, pl.ds(0, 8 * (s.light - 1))], spz.at[i])
+        wait(recv_py.at[i, pl.ds(0, s.heavy - 1)], spy.at[i])
+    left(lambda j: gain_own.at[j], sw.at[0])
+    left(lambda j: w2_in.at[j], sw.at[1])
 
 
 def local(
@@ -607,37 +647,38 @@
         row(lift_gain), row(lift_bias), row(bias_one), row(bias_two), row(readout),
         local_one, local_two, tx, txk, tx3, txt3, tz3, tzt3, twice,
     ]
-    far = [spec_one.reshape(s.modes, 4096), spec_two.reshape(s.modes, 4096), ty3, tyt3, tza, ma, ym, expand]
+    far = [spec_one.reshape(s.modes, 4096), spec_two.reshape(2, s.kz, 4096), ty3, tyt3, tza, ma, ym, expand]
     f32, bf16 = jnp.float32, jnp.bfloat16
     vmem = lambda *dims: pltpu.VMEM(dims, f32)
     half = s.kx * s.rows
     cell = (PIECES, 128, 128 * s.deep)
     scratch = [
         vmem(UNITS, half, 128), vmem(UNITS, half, 128),
-        vmem(UNITS, s.gz, 2, 128), vmem(UNITS, s.gz, 2, 128),
-        vmem(3, s.gz, 4, 128), vmem(3, s.gz, 4, 128),
-        vmem(3, 8, 128), vmem(3, s.gy, 8, 128),
-        vmem(s.gy, 8, 128), vmem(s.gy, 8, 128),
-        vmem(2, 4, 128), vmem(s.gz, 4, 128),
-        vmem(2, s.gz, 2, 128), vmem(2, s.gz, 2, 128),
-        vmem(2, s.gy, 8, 128), vmem(2, s.gy, 8, 128),
+        vmem(UNITS, 8 * s.light, 128), vmem(UNITS, 8 * s.light, 128),
+        vmem(3, s.light, 16, 128), vmem(3, s.light, 16, 128),
+        vmem(3, 2, 128), vmem(3, s.heavy, 2, 128),
+        vmem(s.heavy, 2, 128), vmem(s.heavy, 2, 128),
+        vmem(8, 128), vmem(8 * s.light, 128),
+        vmem(2, 8 * s.light, 128), vmem(2, 8 * s.light, 128),
+        vmem(2, s.gy, 2, 128), vmem(2, s.heavy, 2, 128),
         pltpu.VMEM((5, 384, 128), bf16),
-    ] + [vmem(*cell) for _ in range(10)] + [vmem(2, 2 * s.rows, 128), vmem(8, 64)]
+    ] + [vmem(*cell) for _ in range(10)] + [vmem(2, 2 * s.rows, 128), vmem(8, 64), vmem(128, 128)]
+    scratch += [vmem(2, s.kz, 128), vmem(2, s.kz, 128)]
     scratch += [pltpu.VMEM(x.shape, x.dtype) for x in far]
-    counts = [(UNITS,), (UNITS, PIECES), (UNITS,), (UNITS,), (3,), (3,), (2,), (2,), (2,), (2,), (2,), (2,), (len(far),)]
+    counts = [(UNITS,), (UNITS, PIECES), (UNITS,), (UNITS,), (3,), (3,), (2,), (2,), (2,), (2,), (2,), (2,), (2,), (2,), (len(far),)]
     scratch += [pltpu.SemaphoreType.DMA(n) for n in counts]
-    results = pl.pallas_call(
+    result = pl.pallas_call(
         functools.partial(kernel, s),
-        out_shape=[jax.ShapeDtypeStruct((2 * s.rows, s.line), f32)] * 2,
+        out_shape=jax.ShapeDtypeStruct((2, 2 * s.rows, s.line), f32),
         in_specs=[pl.BlockSpec(memory_space=pltpu.VMEM)] * len(near) + [pl.BlockSpec(memory_space=pl.ANY)] * len(far),
-        out_specs=[pl.BlockSpec(memory_space=pltpu.VMEM)] * 2,
+        out_specs=pl.BlockSpec(memory_space=pltpu.VMEM),
         scratch_shapes=scratch,
         compiler_params=pltpu.CompilerParams(
             collective_id=0, has_side_effects=True, vmem_limit_bytes=60 * 1024 * 1024
         ),
         name="two_steps",
     )(*near, *far)
-    return tuple(x.reshape(shape) for x in results)
+    return tuple(result[i].reshape(shape) for i in range(2))
 
 
 def solution(mesh, kx=KX, ky=KY, kz=KZ, rows=16, line=128):

time: 226 us -> 218 us (0.965)
  Pallas kernels: 223 us -> 216 us
    pallas_call x1, Pallas kernels: 223 us -> 216 us  [local(): pl.pallas_call(functools.partial(kernel, s), out_shape=jax.ShapeDtypeStru...]
where the time goes in v3:
time: 218 us
  Pallas kernels  216 us (99%)
    pallas_call x1, Pallas kernels, local(): pl.pallas_call(functools.partial(kernel, s), out_shape=jax.ShapeDtypeStru...  216 us

profile of v3, /device:TPU:1, one launch (start us, length us, event | category | flops | bytes accessed | tf_op | source)
XLA Modules:
  0.0 217.9 jit_solution(17842307388555190900)
XLA Ops:
  0.6 216.0 %two_steps.1 = f32[2,32,128]{2,1,0:T(8,128)} custom-call(f32[32,128]{1,0:T(8,128)} %bitcast.14, f32[32,128]{1,0:T(8,128)} %bitcast.15, f32[32,128]{1,0:T(8,128)} %bitcast.16, f32[1,64]{1,0:T(1,128)} %bitcast.19, f32[1,64]{1,0:T(1,128)} %bitcast.20, f32[1,64]{1,0:T(1,128)} %bitcast.21, f32[1,64]{1,0:T(1,128)} %bitcast.22, f32[1,64]{1,0:T(1,128)} %bitcast.23, ...), custom_call_target="tpu_custom_call" | custom-call | tf_op jit(solution)/shard_map/two_steps/pallas_call | solution.py:670
  216.6 1.3 fusion

commit v4 on v3

--- a/solution.py
+++ b/solution.py
@@ -546,8 +546,10 @@
     cells_y(F0)
     for p in range(PIECES):
         value = slope_one[p] * (cells_x(F0, p) + mat(mix_back, split(back[p])))
-        parts = split(value)
-        modes_x(G0, p, parts)
+        act[p] = value
+        modes_x(G0, p, split(value))
+    for p in range(PIECES):
+        parts = split(act[p])
         local_rows(0, p, parts)
         qb[p] = rb[p] * (1.0 - DAMPING * step_zero) - step_zero * mat(lift_mat, parts)
     modes_y(G0)
@@ -594,9 +596,10 @@
     cells_y(F1)
     for p in range(PIECES):
         value = slope_one[p] * (cells_x(F1, p) + mat(mix_back, split(back[p])))
-        parts = split(value)
-        modes_x(G1, p, parts)
-        local_rows(1, p, parts)
+        act[p] = value
+        modes_x(G1, p, split(value))
+    for p in range(PIECES):
+        local_rows(1, p, split(act[p]))
     modes_y(G1)
     values, _ = modes_z(G1)
     scalar_z(1, jnp.sum(values * gain_mix * low_half, axis=1, keepdims=True))

time: 218 us -> 218 us (level)
  no operation moved by 1% of the time
where the time goes in v4:
time: 218 us
  Pallas kernels  216 us (99%)
    pallas_call x1, Pallas kernels, local(): pl.pallas_call(functools.partial(kernel, s), out_shape=jax.ShapeDtypeStru...  216 us

profile of v4, /device:TPU:1, one launch (start us, length us, event | category | flops | bytes accessed | tf_op | source)
XLA Modules:
  0.0 218.1 jit_solution(7954438324037096263)
XLA Ops:
  0.6 216.1 %two_steps.1 = f32[2,32,128]{2,1,0:T(8,128)} custom-call(f32[32,128]{1,0:T(8,128)} %bitcast.14, f32[32,128]{1,0:T(8,128)} %bitcast.15, f32[32,128]{1,0:T(8,128)} %bitcast.16, f32[1,64]{1,0:T(1,128)} %bitcast.19, f32[1,64]{1,0:T(1,128)} %bitcast.20, f32[1,64]{1,0:T(1,128)} %bitcast.21, f32[1,64]{1,0:T(1,128)} %bitcast.22, f32[1,64]{1,0:T(1,128)} %bitcast.23, ...), custom_call_target="tpu_custom_call" | custom-call | tf_op jit(solution)/shard_map/two_steps/pallas_call | solution.py:673
  216.7 1.3 fusion
